TPU v7x, 256 devices: a whole 4x4x8 slice. The times are simulated.
256 devices in a mesh: grow: 64 (over y, x_hi, z), lat: 4 (over x_lo, core).
Axes of the slice: x: 4 (x_hi: 2, x_lo: 2; x = x_hi * 2 + x_lo), y: 4, z: 8, core: 2. Of those that a mesh axis runs over, the one named last changes fastest.
Arguments:
- labels: int32 [1024, 128, 128], P('grow', 'lat'), may hold values from 0 to 3
- roughness: float32 [4, 1024, 128, 128], P(None, 'grow', 'lat'), may hold values from 0.1 to 1
- potential: float32 [2, 1024, 128, 128], P(None, 'grow', 'lat'), may hold values from -3 to 3
- grad_coef: float32 [4, 3], replicated, may hold values from 0.2 to 1
- composition: float32 [4, 2], replicated, may hold values from -2 to 2
- latent: float32 [4], replicated, may hold values from 0.5 to 2
- diffusivity: float32 [2], replicated, may hold values from 0.5 to 2
- melt_table: float32 [16, 2], replicated, may hold values from -1 to 1
- melt_index: int32 [4, 8, 128, 128], P(None, None, 'lat'), may hold values from 0 to 15
Outputs:
- phases: float32 [4, 1024, 128, 128], P(None, 'grow', 'lat')
- potentials: float32 [2, 1024, 128, 128], P(None, 'grow', 'lat')
All inputs are finite; a program needn't handle non-finite values.
Results may differ from a plain program's by a relative error of at most 0.00025.
Values sent between devices are 32-bit elements; how exact they have to be, the bound alone decides.
A program may use at most 64 MiB of HBM per device.

v0:
```python
import jax
import jax.numpy as jnp
from jax import lax
from jax.sharding import PartitionSpec as P

STEPS = 4
ROUNDS = 4
SHIFT = 8


def padded_2(array, sides, width):
    edges = {}
    for axis, dim in sides:
        peers, length = (lax.axis_size(axis), array.shape[dim])
        up = [(i, (i + 1) % peers) for i in range(peers)]
        last = lax.slice_in_dim(array, length - width, length, axis=dim)
        leading = lax.slice_in_dim(array, 0, width, axis=dim)
        edges[dim] = (
            lax.ppermute(last, axis, up),
            lax.ppermute(leading, axis, [(b, a) for a, b in up]),
        )
    done = []
    for _, dim in sides:
        low, high = edges[dim]
        around = [(width, width) if d in done else (0, 0) for d in range(array.ndim)]
        array = jnp.concatenate([jnp.pad(low, around), array, jnp.pad(high, around)], axis=dim)
        done.append(dim)
    return array


def passed_along(block, axis, distance):
    devices = range(lax.axis_size(axis))
    route = [(i - distance, i) for i in devices if i - distance in devices]
    return lax.ppermute(block, axis, route)


def advance(padded, grad_coef, composition, latent, diffusivity, first, total):
    center = padded[:, 1:-1, 1:-1]
    gsum = padded[:, 2:, 1:-1] + padded[:, :-2, 1:-1] - 2.0 * center
    xsum = padded[:, 1:-1, 2:] + padded[:, 1:-1, :-2] - 2.0 * center
    ysum = jnp.roll(center, 1, 3) + jnp.roll(center, -1, 3) - 2.0 * center
    fracs = center[:4]
    chem = center[4:]
    lap_phi = (
        grad_coef[:, 0][:, None, None, None] * gsum[:4]
        + grad_coef[:, 1][:, None, None, None] * xsum[:4]
        + grad_coef[:, 2][:, None, None, None] * ysum[:4]
    )
    lap_mu = gsum[4:] + xsum[4:] + ysum[4:]
    rows = center.shape[1]
    theta = ((jnp.arange(rows, dtype=jnp.int32) + first).astype(jnp.float32) - 0.5 * total) / total
    psi = (
        composition[:, 0][:, None, None, None] * chem[0]
        + composition[:, 1][:, None, None, None] * chem[1]
        + latent[:, None, None, None] * theta[None, :, None, None]
    )
    summed = jnp.sum(fracs, axis=0)
    rhs = lap_phi - 1.0 * (summed[None] - fracs) - psi
    rhs = rhs - jnp.mean(rhs, axis=0)[None]
    trial = fracs + 0.04 * rhs
    clipped = jnp.clip(trial, 0.0, 1.0)
    newphi = clipped / jnp.sum(clipped, axis=0)[None]
    change = newphi - fracs
    release = jnp.stack(
        [
            jnp.sum(composition[:, 0][:, None, None, None] * change, axis=0),
            jnp.sum(composition[:, 1][:, None, None, None] * change, axis=0),
        ]
    )
    newmu = chem + 0.04 * diffusivity[:, None, None, None] * lap_mu - release
    return jnp.concatenate([newphi, newmu], axis=0)


def settle(padded, margin, block):
    place = lax.axis_index("grow")
    final = lax.axis_size("grow") - 1
    rows = lax.broadcasted_iota(jnp.int32, (1, padded.shape[1], 1, 1), 1)
    lower = padded[:, margin : margin + 1]
    upper = padded[:, margin + block - 1 : margin + block]
    out = jnp.where((place == 0) & (rows < margin), lower, padded)
    return jnp.where((place == final) & (rows >= margin + block), upper, out)


def melt_planes(melt_table, melt_index, turn):
    rowsmelt = melt_table.shape[0]
    table_cols = jnp.transpose(melt_table)
    chosen = lax.dynamic_index_in_dim(melt_index, turn, 0, keepdims=False)
    entries = jnp.arange(rowsmelt, dtype=jnp.int32)[:, None, None, None]
    picks = (chosen[None] == entries).astype(jnp.float32)
    melt_mu = jnp.tensordot(table_cols, picks, axes=1, precision=lax.Precision.HIGHEST)
    zeros = jnp.zeros(chosen.shape, jnp.float32)
    return jnp.concatenate([jnp.stack([zeros, zeros, zeros, zeros + 1.0]), melt_mu], axis=0)


def on_device(
    labels,
    roughness,
    potential,
    grad_coef,
    composition,
    latent,
    diffusivity,
    melt_table,
    melt_index,
):
    block = labels.shape[0]
    total = float(block * lax.axis_size("grow"))
    place = lax.axis_index("grow")
    final = lax.axis_size("grow") - 1
    kinds = jnp.arange(4, dtype=jnp.int32)[:, None, None, None]
    onehot = (labels[None] == kinds).astype(jnp.float32)
    fracs = (3.0 * onehot + roughness) / (3.0 + jnp.sum(roughness, axis=0))[None]
    start = jnp.concatenate([fracs, potential], axis=0)

    def one_round(turn, state):
        base = place * block + SHIFT * turn
        fresh = melt_planes(melt_table, melt_index, turn)
        for step in range(STEPS):
            padded = padded_2(state, (("grow", 1), ("lat", 2)), 1)
            padded = settle(padded, 1, block)
            state = advance(padded, grad_coef, composition, latent, diffusivity, base, total)
        incoming = passed_along(state[:, :SHIFT], "grow", -1)
        incoming = jnp.where(place == final, fresh, incoming)
        return jnp.concatenate([state[:, SHIFT:], incoming], axis=1)

    state = lax.fori_loop(0, ROUNDS, one_round, start)
    return (state[:4], state[4:])


def solution(mesh):
    placed = (
        P("grow", "lat", None),
        P(None, "grow", "lat", None),
        P(None, "grow", "lat", None),
        P(),
        P(),
        P(),
        P(),
        P(),
        P(None, None, "lat", None),
    )
    return jax.shard_map(
        on_device,
        mesh=mesh,
        in_specs=placed,
        out_specs=(P(None, "grow", "lat", None), P(None, "grow", "lat", None)),
        check_vma=False,
    )
```

profile of v0, /device:TPU:249, one launch (start us, length us, event | category | flops | bytes accessed | tf_op | source)
XLA Modules:
  0.0 480.1 jit_solution(1788881587890463687)
XLA Ops:
  5.4 472.2 %while.15 = (s32[]{:T(128)}, f32[6,16,32,128]{3,0,2,1:T(8,128)S(1)}, f32[4,3]{0,1:T(4,128)S(1)}, f32[4,2]{0,1:T(2,128)S(1)}, f32[4]{0:T(128)S(1)}, /*index=5*/s3...) while((s32[]{:T(128)}, ...), condition=%wide.region_22.23_spmd, body=%wide.region_1.22_spmd.sunk | while | flops 96127200 | bytes 218166240 | solution.py:126
  6.7 4.4 collective-permute-start.3
  12.4 3.8 collective-permute-start.1
  29.8 4.4 collective-permute-start.7
  51.7 5.1 %collective-permute-start.11 = (f32[6,1,32,128]{3,0,2,1:T(8,128)S(1)}, f32[6,1,32,128]{3,0,2,1:T(8,128)S(1)}, u32[]{:S(2)}, u32[]{:S(2)}) collective-permute-start(f32[6,1,32,128]{3,0,2,1:T(8,128)S(1)} %get-tuple-element.563), channel_id=1, source_target_pairs={{0,4},{4,8},{8,12},{12,16},{16,20},{20,24},{24,28},{28,32},{32,36}... | collective-permute-start | bytes 294920 | tf_op jit(solution)/shard_map/while/body/eval_jaxpr/ppermute | solution.py:19
  59.5 3.4 collective-permute-done.8
  74.7 5.1 %collective-permute-start.15 = (f32[6,1,32,128]{3,0,2,1:T(8,128)S(1)}, f32[6,1,32,128]{3,0,2,1:T(8,128)S(1)}, u32[]{:S(2)}, u32[]{:S(2)}) collective-permute-start(f32[6,1,32,128]{3,0,2,1:T(8,128)S(1)} %get-tuple-element.583), channel_id=1, source_target_pairs={{0,4},{4,8},{8,12},{12,16},{16,20},{20,24},{24,28},{28,32},{32,36}... | collective-permute-start | bytes 294920 | tf_op jit(solution)/shard_map/while/body/eval_jaxpr/ppermute | solution.py:19
  100.4 20.4 %collective-permute-done.16 = f32[6,8,32,128]{3,2,1,0:T(8,128)S(1)} collective-permute-done((f32[6,8,32,128]{3,2,1,0:T(8,128)S(1)}, f32[6,8,32,128]{3,2,1,0:T(8,128)S(1)}, u32[]{:S(2)}, u32[]{:S(2)}) %collective-permute-start.16) | collective-permute-done | bytes 786464 | tf_op jit(solution)/shard_map/while/body/eval_jaxpr/ppermute | solution.py:34
  122.1 5.1 %collective-permute-start.3 = (f32[6,1,32,128]{3,0,2,1:T(8,128)S(1)}, f32[6,1,32,128]{3,0,2,1:T(8,128)S(1)}, u32[]{:S(2)}, u32[]{:S(2)}) collective-permute-start(f32[6,1,32,128]{3,0,2,1:T(8,128)S(1)} %get-tuple-element.517), channel_id=1, source_target_pairs={{0,4},{4,8},{8,12},{12,16},{16,20},{20,24},{24,28},{28,32},{32,36}... | collective-permute-start | bytes 294920 | tf_op jit(solution)/shard_map/while/body/eval_jaxpr/ppermute | solution.py:19
  129.3 4.2 collective-permute-start.1
  146.3 5.1 %collective-permute-start.7 = (f32[6,1,32,128]{3,0,2,1:T(8,128)S(1)}, f32[6,1,32,128]{3,0,2,1:T(8,128)S(1)}, u32[]{:S(2)}, u32[]{:S(2)}) collective-permute-start(f32[6,1,32,128]{3,0,2,1:T(8,128)S(1)} %get-tuple-element.543), channel_id=1, source_target_pairs={{0,4},{4,8},{8,12},{12,16},{16,20},{20,24},{24,28},{28,32},{32,36}... | collective-permute-start | bytes 294920 | tf_op jit(solution)/shard_map/while/body/eval_jaxpr/ppermute | solution.py:19
  154.9 3.3 collective-permute-done.4
  170.1 5.1 %collective-permute-start.11 = (f32[6,1,32,128]{3,0,2,1:T(8,128)S(1)}, f32[6,1,32,128]{3,0,2,1:T(8,128)S(1)}, u32[]{:S(2)}, u32[]{:S(2)}) collective-permute-start(f32[6,1,32,128]{3,0,2,1:T(8,128)S(1)} %get-tuple-element.563), channel_id=1, source_target_pairs={{0,4},{4,8},{8,12},{12,16},{16,20},{20,24},{24,28},{28,32},{32,36}... | collective-permute-start | bytes 294920 | tf_op jit(solution)/shard_map/while/body/eval_jaxpr/ppermute | solution.py:19
  177.3 3.6 collective-permute-done.8
  192.8 5.1 %collective-permute-start.15 = (f32[6,1,32,128]{3,0,2,1:T(8,128)S(1)}, f32[6,1,32,128]{3,0,2,1:T(8,128)S(1)}, u32[]{:S(2)}, u32[]{:S(2)}) collective-permute-start(f32[6,1,32,128]{3,0,2,1:T(8,128)S(1)} %get-tuple-element.583), channel_id=1, source_target_pairs={{0,4},{4,8},{8,12},{12,16},{16,20},{20,24},{24,28},{28,32},{32,36}... | collective-permute-start | bytes 294920 | tf_op jit(solution)/shard_map/while/body/eval_jaxpr/ppermute | solution.py:19
  218.6 20.6 %collective-permute-done.16 = f32[6,8,32,128]{3,2,1,0:T(8,128)S(1)} collective-permute-done((f32[6,8,32,128]{3,2,1,0:T(8,128)S(1)}, f32[6,8,32,128]{3,2,1,0:T(8,128)S(1)}, u32[]{:S(2)}, u32[]{:S(2)}) %collective-permute-start.16) | collective-permute-done | bytes 786464 | tf_op jit(solution)/shard_map/while/body/eval_jaxpr/ppermute | solution.py:34
  240.6 5.1 %collective-permute-start.3 = (f32[6,1,32,128]{3,0,2,1:T(8,128)S(1)}, f32[6,1,32,128]{3,0,2,1:T(8,128)S(1)}, u32[]{:S(2)}, u32[]{:S(2)}) collective-permute-start(f32[6,1,32,128]{3,0,2,1:T(8,128)S(1)} %get-tuple-element.517), channel_id=1, source_target_pairs={{0,4},{4,8},{8,12},{12,16},{16,20},{20,24},{24,28},{28,32},{32,36}... | collective-permute-start | bytes 294920 | tf_op jit(solution)/shard_map/while/body/eval_jaxpr/ppermute | solution.py:19
  247.5 3.9 collective-permute-start.1
  264.3 5.1 %collective-permute-start.7 = (f32[6,1,32,128]{3,0,2,1:T(8,128)S(1)}, f32[6,1,32,128]{3,0,2,1:T(8,128)S(1)}, u32[]{:S(2)}, u32[]{:S(2)}) collective-permute-start(f32[6,1,32,128]{3,0,2,1:T(8,128)S(1)} %get-tuple-element.543), channel_id=1, source_target_pairs={{0,4},{4,8},{8,12},{12,16},{16,20},{20,24},{24,28},{28,32},{32,36}... | collective-permute-start | bytes 294920 | tf_op jit(solution)/shard_map/while/body/eval_jaxpr/ppermute | solution.py:19
  272.9 3.4 collective-permute-done.4
  288.2 5.1 %collective-permute-start.11 = (f32[6,1,32,128]{3,0,2,1:T(8,128)S(1)}, f32[6,1,32,128]{3,0,2,1:T(8,128)S(1)}, u32[]{:S(2)}, u32[]{:S(2)}) collective-permute-start(f32[6,1,32,128]{3,0,2,1:T(8,128)S(1)} %get-tuple-element.563), channel_id=1, source_target_pairs={{0,4},{4,8},{8,12},{12,16},{16,20},{20,24},{24,28},{28,32},{32,36}... | collective-permute-start | bytes 294920 | tf_op jit(solution)/shard_map/while/body/eval_jaxpr/ppermute | solution.py:19
  295.4 3.7 collective-permute-done.8
  310.9 5.1 %collective-permute-start.15 = (f32[6,1,32,128]{3,0,2,1:T(8,128)S(1)}, f32[6,1,32,128]{3,0,2,1:T(8,128)S(1)}, u32[]{:S(2)}, u32[]{:S(2)}) collective-permute-start(f32[6,1,32,128]{3,0,2,1:T(8,128)S(1)} %get-tuple-element.583), channel_id=1, source_target_pairs={{0,4},{4,8},{8,12},{12,16},{16,20},{20,24},{24,28},{28,32},{32,36}... | collective-permute-start | bytes 294920 | tf_op jit(solution)/shard_map/while/body/eval_jaxpr/ppermute | solution.py:19
  336.7 20.6 %collective-permute-done.16 = f32[6,8,32,128]{3,2,1,0:T(8,128)S(1)} collective-permute-done((f32[6,8,32,128]{3,2,1,0:T(8,128)S(1)}, f32[6,8,32,128]{3,2,1,0:T(8,128)S(1)}, u32[]{:S(2)}, u32[]{:S(2)}) %collective-permute-start.16) | collective-permute-done | bytes 786464 | tf_op jit(solution)/shard_map/while/body/eval_jaxpr/ppermute | solution.py:34
  358.7 5.1 %collective-permute-start.3 = (f32[6,1,32,128]{3,0,2,1:T(8,128)S(1)}, f32[6,1,32,128]{3,0,2,1:T(8,128)S(1)}, u32[]{:S(2)}, u32[]{:S(2)}) collective-permute-start(f32[6,1,32,128]{3,0,2,1:T(8,128)S(1)} %get-tuple-element.517), channel_id=1, source_target_pairs={{0,4},{4,8},{8,12},{12,16},{16,20},{20,24},{24,28},{28,32},{32,36}... | collective-permute-start | bytes 294920 | tf_op jit(solution)/shard_map/while/body/eval_jaxpr/ppermute | solution.py:19
  365.6 3.9 collective-permute-start.1
  382.4 5.1 %collective-permute-start.7 = (f32[6,1,32,128]{3,0,2,1:T(8,128)S(1)}, f32[6,1,32,128]{3,0,2,1:T(8,128)S(1)}, u32[]{:S(2)}, u32[]{:S(2)}) collective-permute-start(f32[6,1,32,128]{3,0,2,1:T(8,128)S(1)} %get-tuple-element.543), channel_id=1, source_target_pairs={{0,4},{4,8},{8,12},{12,16},{16,20},{20,24},{24,28},{28,32},{32,36}... | collective-permute-start | bytes 294920 | tf_op jit(solution)/shard_map/while/body/eval_jaxpr/ppermute | solution.py:19
  391.0 3.4 collective-permute-done.4
  406.3 5.1 %collective-permute-start.11 = (f32[6,1,32,128]{3,0,2,1:T(8,128)S(1)}, f32[6,1,32,128]{3,0,2,1:T(8,128)S(1)}, u32[]{:S(2)}, u32[]{:S(2)}) collective-permute-start(f32[6,1,32,128]{3,0,2,1:T(8,128)S(1)} %get-tuple-element.563), channel_id=1, source_target_pairs={{0,4},{4,8},{8,12},{12,16},{16,20},{20,24},{24,28},{28,32},{32,36}... | collective-permute-start | bytes 294920 | tf_op jit(solution)/shard_map/while/body/eval_jaxpr/ppermute | solution.py:19
  413.5 3.7 collective-permute-done.8
  429.0 5.1 %collective-permute-start.15 = (f32[6,1,32,128]{3,0,2,1:T(8,128)S(1)}, f32[6,1,32,128]{3,0,2,1:T(8,128)S(1)}, u32[]{:S(2)}, u32[]{:S(2)}) collective-permute-start(f32[6,1,32,128]{3,0,2,1:T(8,128)S(1)} %get-tuple-element.583), channel_id=1, source_target_pairs={{0,4},{4,8},{8,12},{12,16},{16,20},{20,24},{24,28},{28,32},{32,36}... | collective-permute-start | bytes 294920 | tf_op jit(solution)/shard_map/while/body/eval_jaxpr/ppermute | solution.py:19
  454.8 20.6 %collective-permute-done.16 = f32[6,8,32,128]{3,2,1,0:T(8,128)S(1)} collective-permute-done((f32[6,8,32,128]{3,2,1,0:T(8,128)S(1)}, f32[6,8,32,128]{3,2,1,0:T(8,128)S(1)}, u32[]{:S(2)}, u32[]{:S(2)}) %collective-permute-start.16) | collective-permute-done | bytes 786464 | tf_op jit(solution)/shard_map/while/body/eval_jaxpr/ppermute | solution.py:34
  (400 shorter events, 271.9 us)
Async XLA Ops:
  5.9 11.6 %collective-permute-start.2 = (f32[6,1,32,128]{3,0,2,1:T(8,128)S(1)}, f32[6,1,32,128]{3,0,2,1:T(8,128)S(1)}, u32[]{:S(2)}, u32[]{:S(2)}) collective-permute-start(f32[6,1,32,128]{3,0,2,1:T(8,128)S(1)} %get-tuple-element.516), channel_id=1, source_target_pairs={{4,0},{8,4},{12,8},{16,12},{20,16},{24,20},{28,24},{32,28},{36,32}... | collective-permute-start | bytes 294920 | tf_op jit(solution)/shard_map/while/body/eval_jaxpr/ppermute | solution.py:20
  6.7 10.8 %collective-permute-start.3 = (f32[6,1,32,128]{3,0,2,1:T(8,128)S(1)}, f32[6,1,32,128]{3,0,2,1:T(8,128)S(1)}, u32[]{:S(2)}, u32[]{:S(2)}) collective-permute-start(f32[6,1,32,128]{3,0,2,1:T(8,128)S(1)} %get-tuple-element.517), channel_id=1, source_target_pairs={{0,4},{4,8},{8,12},{12,16},{16,20},{20,24},{24,28},{28,32},{32,36}... | collective-permute-start | bytes 294920 | tf_op jit(solution)/shard_map/while/body/eval_jaxpr/ppermute | solution.py:19
  29.0 10.9 %collective-permute-start.6 = (f32[6,1,32,128]{3,0,2,1:T(8,128)S(1)}, f32[6,1,32,128]{3,0,2,1:T(8,128)S(1)}, u32[]{:S(2)}, u32[]{:S(2)}) collective-permute-start(f32[6,1,32,128]{3,0,2,1:T(8,128)S(1)} %get-tuple-element.542), channel_id=1, source_target_pairs={{4,0},{8,4},{12,8},{16,12},{20,16},{24,20},{28,24},{32,28},{36,32}... | collective-permute-start | bytes 294920 | tf_op jit(solution)/shard_map/while/body/eval_jaxpr/ppermute | solution.py:20
  51.6 11.2 %collective-permute-start.10 = (f32[6,1,32,128]{3,0,2,1:T(8,128)S(1)}, f32[6,1,32,128]{3,0,2,1:T(8,128)S(1)}, u32[]{:S(2)}, u32[]{:S(2)}) collective-permute-start(f32[6,1,32,128]{3,0,2,1:T(8,128)S(1)} %get-tuple-element.562), channel_id=1, source_target_pairs={{4,0},{8,4},{12,8},{16,12},{20,16},{24,20},{28,24},{32,28},{36,32}... | collective-permute-start | bytes 294920 | tf_op jit(solution)/shard_map/while/body/eval_jaxpr/ppermute | solution.py:20
  51.7 11.1 %collective-permute-start.11 = (f32[6,1,32,128]{3,0,2,1:T(8,128)S(1)}, f32[6,1,32,128]{3,0,2,1:T(8,128)S(1)}, u32[]{:S(2)}, u32[]{:S(2)}) collective-permute-start(f32[6,1,32,128]{3,0,2,1:T(8,128)S(1)} %get-tuple-element.563), channel_id=1, source_target_pairs={{0,4},{4,8},{8,12},{12,16},{16,20},{20,24},{24,28},{28,32},{32,36}... | collective-permute-start | bytes 294920 | tf_op jit(solution)/shard_map/while/body/eval_jaxpr/ppermute | solution.py:19
  96.7 24.0 %collective-permute-start.16 = (f32[6,8,32,128]{3,2,1,0:T(8,128)S(1)}, f32[6,8,32,128]{3,2,1,0:T(8,128)S(1)}, u32[]{:S(2)}, u32[]{:S(2)}) collective-permute-start(f32[6,8,32,128]{3,2,1,0:T(8,128)S(1)} %copy.31), channel_id=1, source_target_pairs={{4,0},{8,4},{12,8},{16,12},{20,16},{24,20},{28,24},{32,28},{36,32}... | collective-permute-start | bytes 2359304 | tf_op jit(solution)/shard_map/while/body/eval_jaxpr/ppermute | solution.py:34
  122.0 12.8 %collective-permute-start.2 = (f32[6,1,32,128]{3,0,2,1:T(8,128)S(1)}, f32[6,1,32,128]{3,0,2,1:T(8,128)S(1)}, u32[]{:S(2)}, u32[]{:S(2)}) collective-permute-start(f32[6,1,32,128]{3,0,2,1:T(8,128)S(1)} %get-tuple-element.516), channel_id=1, source_target_pairs={{4,0},{8,4},{12,8},{16,12},{20,16},{24,20},{28,24},{32,28},{36,32}... | collective-permute-start | bytes 294920 | tf_op jit(solution)/shard_map/while/body/eval_jaxpr/ppermute | solution.py:20
  122.1 12.7 %collective-permute-start.3 = (f32[6,1,32,128]{3,0,2,1:T(8,128)S(1)}, f32[6,1,32,128]{3,0,2,1:T(8,128)S(1)}, u32[]{:S(2)}, u32[]{:S(2)}) collective-permute-start(f32[6,1,32,128]{3,0,2,1:T(8,128)S(1)} %get-tuple-element.517), channel_id=1, source_target_pairs={{0,4},{4,8},{8,12},{12,16},{16,20},{20,24},{24,28},{28,32},{32,36}... | collective-permute-start | bytes 294920 | tf_op jit(solution)/shard_map/while/body/eval_jaxpr/ppermute | solution.py:19
  146.2 12.0 %collective-permute-start.6 = (f32[6,1,32,128]{3,0,2,1:T(8,128)S(1)}, f32[6,1,32,128]{3,0,2,1:T(8,128)S(1)}, u32[]{:S(2)}, u32[]{:S(2)}) collective-permute-start(f32[6,1,32,128]{3,0,2,1:T(8,128)S(1)} %get-tuple-element.542), channel_id=1, source_target_pairs={{4,0},{8,4},{12,8},{16,12},{20,16},{24,20},{28,24},{32,28},{36,32}... | collective-permute-start | bytes 294920 | tf_op jit(solution)/shard_map/while/body/eval_jaxpr/ppermute | solution.py:20
  146.3 11.9 %collective-permute-start.7 = (f32[6,1,32,128]{3,0,2,1:T(8,128)S(1)}, f32[6,1,32,128]{3,0,2,1:T(8,128)S(1)}, u32[]{:S(2)}, u32[]{:S(2)}) collective-permute-start(f32[6,1,32,128]{3,0,2,1:T(8,128)S(1)} %get-tuple-element.543), channel_id=1, source_target_pairs={{0,4},{4,8},{8,12},{12,16},{16,20},{20,24},{24,28},{28,32},{32,36}... | collective-permute-start | bytes 294920 | tf_op jit(solution)/shard_map/while/body/eval_jaxpr/ppermute | solution.py:19
  170.0 10.9 %collective-permute-start.10 = (f32[6,1,32,128]{3,0,2,1:T(8,128)S(1)}, f32[6,1,32,128]{3,0,2,1:T(8,128)S(1)}, u32[]{:S(2)}, u32[]{:S(2)}) collective-permute-start(f32[6,1,32,128]{3,0,2,1:T(8,128)S(1)} %get-tuple-element.562), channel_id=1, source_target_pairs={{4,0},{8,4},{12,8},{16,12},{20,16},{24,20},{28,24},{32,28},{36,32}... | collective-permute-start | bytes 294920 | tf_op jit(solution)/shard_map/while/body/eval_jaxpr/ppermute | solution.py:20
  170.1 10.8 %collective-permute-start.11 = (f32[6,1,32,128]{3,0,2,1:T(8,128)S(1)}, f32[6,1,32,128]{3,0,2,1:T(8,128)S(1)}, u32[]{:S(2)}, u32[]{:S(2)}) collective-permute-start(f32[6,1,32,128]{3,0,2,1:T(8,128)S(1)} %get-tuple-element.563), channel_id=1, source_target_pairs={{0,4},{4,8},{8,12},{12,16},{16,20},{20,24},{24,28},{28,32},{32,36}... | collective-permute-start | bytes 294920 | tf_op jit(solution)/shard_map/while/body/eval_jaxpr/ppermute | solution.py:19
  192.7 10.7 %collective-permute-start.14 = (f32[6,1,32,128]{3,0,2,1:T(8,128)S(1)}, f32[6,1,32,128]{3,0,2,1:T(8,128)S(1)}, u32[]{:S(2)}, u32[]{:S(2)}) collective-permute-start(f32[6,1,32,128]{3,0,2,1:T(8,128)S(1)} %get-tuple-element.582), channel_id=1, source_target_pairs={{4,0},{8,4},{12,8},{16,12},{20,16},{24,20},{28,24},{32,28},{36,32}... | collective-permute-start | bytes 294920 | tf_op jit(solution)/shard_map/while/body/eval_jaxpr/ppermute | solution.py:20
  192.8 10.6 %collective-permute-start.15 = (f32[6,1,32,128]{3,0,2,1:T(8,128)S(1)}, f32[6,1,32,128]{3,0,2,1:T(8,128)S(1)}, u32[]{:S(2)}, u32[]{:S(2)}) collective-permute-start(f32[6,1,32,128]{3,0,2,1:T(8,128)S(1)} %get-tuple-element.583), channel_id=1, source_target_pairs={{0,4},{4,8},{8,12},{12,16},{16,20},{20,24},{24,28},{28,32},{32,36}... | collective-permute-start | bytes 294920 | tf_op jit(solution)/shard_map/while/body/eval_jaxpr/ppermute | solution.py:19
  215.0 24.2 %collective-permute-start.16 = (f32[6,8,32,128]{3,2,1,0:T(8,128)S(1)}, f32[6,8,32,128]{3,2,1,0:T(8,128)S(1)}, u32[]{:S(2)}, u32[]{:S(2)}) collective-permute-start(f32[6,8,32,128]{3,2,1,0:T(8,128)S(1)} %copy.31), channel_id=1, source_target_pairs={{4,0},{8,4},{12,8},{16,12},{20,16},{24,20},{28,24},{32,28},{36,32}... | collective-permute-start | bytes 2359304 | tf_op jit(solution)/shard_map/while/body/eval_jaxpr/ppermute | solution.py:34
  240.5 12.3 %collective-permute-start.2 = (f32[6,1,32,128]{3,0,2,1:T(8,128)S(1)}, f32[6,1,32,128]{3,0,2,1:T(8,128)S(1)}, u32[]{:S(2)}, u32[]{:S(2)}) collective-permute-start(f32[6,1,32,128]{3,0,2,1:T(8,128)S(1)} %get-tuple-element.516), channel_id=1, source_target_pairs={{4,0},{8,4},{12,8},{16,12},{20,16},{24,20},{28,24},{32,28},{36,32}... | collective-permute-start | bytes 294920 | tf_op jit(solution)/shard_map/while/body/eval_jaxpr/ppermute | solution.py:20
  240.6 12.2 %collective-permute-start.3 = (f32[6,1,32,128]{3,0,2,1:T(8,128)S(1)}, f32[6,1,32,128]{3,0,2,1:T(8,128)S(1)}, u32[]{:S(2)}, u32[]{:S(2)}) collective-permute-start(f32[6,1,32,128]{3,0,2,1:T(8,128)S(1)} %get-tuple-element.517), channel_id=1, source_target_pairs={{0,4},{4,8},{8,12},{12,16},{16,20},{20,24},{24,28},{28,32},{32,36}... | collective-permute-start | bytes 294920 | tf_op jit(solution)/shard_map/while/body/eval_jaxpr/ppermute | solution.py:19
  264.2 12.1 %collective-permute-start.6 = (f32[6,1,32,128]{3,0,2,1:T(8,128)S(1)}, f32[6,1,32,128]{3,0,2,1:T(8,128)S(1)}, u32[]{:S(2)}, u32[]{:S(2)}) collective-permute-start(f32[6,1,32,128]{3,0,2,1:T(8,128)S(1)} %get-tuple-element.542), channel_id=1, source_target_pairs={{4,0},{8,4},{12,8},{16,12},{20,16},{24,20},{28,24},{32,28},{36,32}... | collective-permute-start | bytes 294920 | tf_op jit(solution)/shard_map/while/body/eval_jaxpr/ppermute | solution.py:20
  264.3 12.0 %collective-permute-start.7 = (f32[6,1,32,128]{3,0,2,1:T(8,128)S(1)}, f32[6,1,32,128]{3,0,2,1:T(8,128)S(1)}, u32[]{:S(2)}, u32[]{:S(2)}) collective-permute-start(f32[6,1,32,128]{3,0,2,1:T(8,128)S(1)} %get-tuple-element.543), channel_id=1, source_target_pairs={{0,4},{4,8},{8,12},{12,16},{16,20},{20,24},{24,28},{28,32},{32,36}... | collective-permute-start | bytes 294920 | tf_op jit(solution)/shard_map/while/body/eval_jaxpr/ppermute | solution.py:19
  288.1 10.9 %collective-permute-start.10 = (f32[6,1,32,128]{3,0,2,1:T(8,128)S(1)}, f32[6,1,32,128]{3,0,2,1:T(8,128)S(1)}, u32[]{:S(2)}, u32[]{:S(2)}) collective-permute-start(f32[6,1,32,128]{3,0,2,1:T(8,128)S(1)} %get-tuple-element.562), channel_id=1, source_target_pairs={{4,0},{8,4},{12,8},{16,12},{20,16},{24,20},{28,24},{32,28},{36,32}... | collective-permute-start | bytes 294920 | tf_op jit(solution)/shard_map/while/body/eval_jaxpr/ppermute | solution.py:20
  288.2 10.8 %collective-permute-start.11 = (f32[6,1,32,128]{3,0,2,1:T(8,128)S(1)}, f32[6,1,32,128]{3,0,2,1:T(8,128)S(1)}, u32[]{:S(2)}, u32[]{:S(2)}) collective-permute-start(f32[6,1,32,128]{3,0,2,1:T(8,128)S(1)} %get-tuple-element.563), channel_id=1, source_target_pairs={{0,4},{4,8},{8,12},{12,16},{16,20},{20,24},{24,28},{28,32},{32,36}... | collective-permute-start | bytes 294920 | tf_op jit(solution)/shard_map/while/body/eval_jaxpr/ppermute | solution.py:19
  310.8 10.7 %collective-permute-start.14 = (f32[6,1,32,128]{3,0,2,1:T(8,128)S(1)}, f32[6,1,32,128]{3,0,2,1:T(8,128)S(1)}, u32[]{:S(2)}, u32[]{:S(2)}) collective-permute-start(f32[6,1,32,128]{3,0,2,1:T(8,128)S(1)} %get-tuple-element.582), channel_id=1, source_target_pairs={{4,0},{8,4},{12,8},{16,12},{20,16},{24,20},{28,24},{32,28},{36,32}... | collective-permute-start | bytes 294920 | tf_op jit(solution)/shard_map/while/body/eval_jaxpr/ppermute | solution.py:20
  310.9 10.6 %collective-permute-start.15 = (f32[6,1,32,128]{3,0,2,1:T(8,128)S(1)}, f32[6,1,32,128]{3,0,2,1:T(8,128)S(1)}, u32[]{:S(2)}, u32[]{:S(2)}) collective-permute-start(f32[6,1,32,128]{3,0,2,1:T(8,128)S(1)} %get-tuple-element.583), channel_id=1, source_target_pairs={{0,4},{4,8},{8,12},{12,16},{16,20},{20,24},{24,28},{28,32},{32,36}... | collective-permute-start | bytes 294920 | tf_op jit(solution)/shard_map/while/body/eval_jaxpr/ppermute | solution.py:19
  333.1 24.2 %collective-permute-start.16 = (f32[6,8,32,128]{3,2,1,0:T(8,128)S(1)}, f32[6,8,32,128]{3,2,1,0:T(8,128)S(1)}, u32[]{:S(2)}, u32[]{:S(2)}) collective-permute-start(f32[6,8,32,128]{3,2,1,0:T(8,128)S(1)} %copy.31), channel_id=1, source_target_pairs={{4,0},{8,4},{12,8},{16,12},{20,16},{24,20},{28,24},{32,28},{36,32}... | collective-permute-start | bytes 2359304 | tf_op jit(solution)/shard_map/while/body/eval_jaxpr/ppermute | solution.py:34
  358.6 12.3 %collective-permute-start.2 = (f32[6,1,32,128]{3,0,2,1:T(8,128)S(1)}, f32[6,1,32,128]{3,0,2,1:T(8,128)S(1)}, u32[]{:S(2)}, u32[]{:S(2)}) collective-permute-start(f32[6,1,32,128]{3,0,2,1:T(8,128)S(1)} %get-tuple-element.516), channel_id=1, source_target_pairs={{4,0},{8,4},{12,8},{16,12},{20,16},{24,20},{28,24},{32,28},{36,32}... | collective-permute-start | bytes 294920 | tf_op jit(solution)/shard_map/while/body/eval_jaxpr/ppermute | solution.py:20
  358.7 12.2 %collective-permute-start.3 = (f32[6,1,32,128]{3,0,2,1:T(8,128)S(1)}, f32[6,1,32,128]{3,0,2,1:T(8,128)S(1)}, u32[]{:S(2)}, u32[]{:S(2)}) collective-permute-start(f32[6,1,32,128]{3,0,2,1:T(8,128)S(1)} %get-tuple-element.517), channel_id=1, source_target_pairs={{0,4},{4,8},{8,12},{12,16},{16,20},{20,24},{24,28},{28,32},{32,36}... | collective-permute-start | bytes 294920 | tf_op jit(solution)/shard_map/while/body/eval_jaxpr/ppermute | solution.py:19
  382.3 12.1 %collective-permute-start.6 = (f32[6,1,32,128]{3,0,2,1:T(8,128)S(1)}, f32[6,1,32,128]{3,0,2,1:T(8,128)S(1)}, u32[]{:S(2)}, u32[]{:S(2)}) collective-permute-start(f32[6,1,32,128]{3,0,2,1:T(8,128)S(1)} %get-tuple-element.542), channel_id=1, source_target_pairs={{4,0},{8,4},{12,8},{16,12},{20,16},{24,20},{28,24},{32,28},{36,32}... | collective-permute-start | bytes 294920 | tf_op jit(solution)/shard_map/while/body/eval_jaxpr/ppermute | solution.py:20
  382.4 12.0 %collective-permute-start.7 = (f32[6,1,32,128]{3,0,2,1:T(8,128)S(1)}, f32[6,1,32,128]{3,0,2,1:T(8,128)S(1)}, u32[]{:S(2)}, u32[]{:S(2)}) collective-permute-start(f32[6,1,32,128]{3,0,2,1:T(8,128)S(1)} %get-tuple-element.543), channel_id=1, source_target_pairs={{0,4},{4,8},{8,12},{12,16},{16,20},{20,24},{24,28},{28,32},{32,36}... | collective-permute-start | bytes 294920 | tf_op jit(solution)/shard_map/while/body/eval_jaxpr/ppermute | solution.py:19
  406.2 10.9 %collective-permute-start.10 = (f32[6,1,32,128]{3,0,2,1:T(8,128)S(1)}, f32[6,1,32,128]{3,0,2,1:T(8,128)S(1)}, u32[]{:S(2)}, u32[]{:S(2)}) collective-permute-start(f32[6,1,32,128]{3,0,2,1:T(8,128)S(1)} %get-tuple-element.562), channel_id=1, source_target_pairs={{4,0},{8,4},{12,8},{16,12},{20,16},{24,20},{28,24},{32,28},{36,32}... | collective-permute-start | bytes 294920 | tf_op jit(solution)/shard_map/while/body/eval_jaxpr/ppermute | solution.py:20
  406.3 10.8 %collective-permute-start.11 = (f32[6,1,32,128]{3,0,2,1:T(8,128)S(1)}, f32[6,1,32,128]{3,0,2,1:T(8,128)S(1)}, u32[]{:S(2)}, u32[]{:S(2)}) collective-permute-start(f32[6,1,32,128]{3,0,2,1:T(8,128)S(1)} %get-tuple-element.563), channel_id=1, source_target_pairs={{0,4},{4,8},{8,12},{12,16},{16,20},{20,24},{24,28},{28,32},{32,36}... | collective-permute-start | bytes 294920 | tf_op jit(solution)/shard_map/while/body/eval_jaxpr/ppermute | solution.py:19
  428.9 10.7 %collective-permute-start.14 = (f32[6,1,32,128]{3,0,2,1:T(8,128)S(1)}, f32[6,1,32,128]{3,0,2,1:T(8,128)S(1)}, u32[]{:S(2)}, u32[]{:S(2)}) collective-permute-start(f32[6,1,32,128]{3,0,2,1:T(8,128)S(1)} %get-tuple-element.582), channel_id=1, source_target_pairs={{4,0},{8,4},{12,8},{16,12},{20,16},{24,20},{28,24},{32,28},{36,32}... | collective-permute-start | bytes 294920 | tf_op jit(solution)/shard_map/while/body/eval_jaxpr/ppermute | solution.py:20
  451.2 24.2 %collective-permute-start.16 = (f32[6,8,32,128]{3,2,1,0:T(8,128)S(1)}, f32[6,8,32,128]{3,2,1,0:T(8,128)S(1)}, u32[]{:S(2)}, u32[]{:S(2)}) collective-permute-start(f32[6,8,32,128]{3,2,1,0:T(8,128)S(1)} %copy.31), channel_id=1, source_target_pairs={{4,0},{8,4},{12,8},{16,12},{20,16},{24,20},{28,24},{32,28},{36,32}... | collective-permute-start | bytes 2359304 | tf_op jit(solution)/shard_map/while/body/eval_jaxpr/ppermute | solution.py:34
  (43 other events, 222.7 us)
where the time goes:
time: 487 us; the launch traced here: 480 us
  other arithmetic  160 us (33%)
  starting transfers between devices  145 us (30%)
  waiting for transfers between devices  127 us (26%)
  local copies, waits for them, and re-layouts  39.9 us (8%)
  loops' own time  4.98 us (1%)
    ppermute x32, starting transfers between devices, padded_2(): lax.ppermute(last, axis, up)  111 us
    ppermute x4, waiting for transfers between devices, passed_along(): return lax.ppermute(block, axis, route)  82.2 us
    ppermute x32, waiting for transfers between devices, padded_2(): lax.ppermute(leading, axis, [(b, a) for a, b in up])  39.8 us
    sub x16, other arithmetic, advance(): rhs = lap_phi - 1.0 * (summed[None] - fracs) - psi  34.8 us
    sub x16, other arithmetic, advance(): gsum = padded[:, 2:, 1:-1] + padded[:, :-2, 1:-1] - 2.0 * center  30.1 us
    ppermute x32, starting transfers between devices, padded_2(): lax.ppermute(leading, axis, [(b, a) for a, b in up])  26.5 us
    reduce_sum x12, other arithmetic, advance(): jnp.sum(composition[:, 0][:, None, None, None] * change, axis=0)  23.4 us
    slice x32, local copies, waits for them, and re-layouts, advance(): ysum = jnp.roll(center, 1, 3) + jnp.roll(center, -1, 3) - 2.0 * center  23.1 us
  transfers between devices with their start and end apart: 68, of which 22 were waited for; matrix products, arithmetic and copies ran while one was open for 2% of the time, Pallas kernels for 0%

commit v1 on v0

v1 whole, which is shorter than its diff:
```python
import functools

import jax
import jax.numpy as jnp
from jax import lax
from jax.experimental import pallas as pl
from jax.experimental.pallas import tpu as pltpu
from jax.sharding import PartitionSpec as P

MESH = pl.DeviceIdType.MESH
STEPS = 4
ROUNDS = 4
SHIFT = 8
DT = 0.04
TOTAL = STEPS * ROUNDS
FIELDS = 5
PAD = 8
AHEAD = 2
HIGH = 16


def kernel(
    peers,
    lats,
    labels,
    rough,
    pot,
    melt_index,
    grad,
    comp,
    latent,
    diff,
    table,
    phases,
    potentials,
    own,
    state,
    odd,
    even,
    z_send,
    z_recv,
    x_send,
    x_recv,
):
    block, rows, cols = labels.shape
    stream = block + 2 * TOTAL
    halo = TOTAL
    low = PAD + halo
    high = low + rows
    planes = peers * block
    p = lax.axis_index("grow")
    q = lax.axis_index("lat")
    below = jnp.maximum(p - 1, 0)
    above = jnp.minimum(p + 1, peers - 1)
    left = lax.rem(q + lats - 1, lats)
    right = lax.rem(q + 1, lats)

    barrier = pltpu.get_barrier_semaphore()
    for side in (left, right):
        pl.semaphore_signal(barrier, inc=1, device_id=(p, side), device_id_type=MESH)

    @pl.when(p < peers - 1)
    def _():
        pl.semaphore_signal(barrier, inc=1, device_id=(above, q), device_id_type=MESH)

    def begin(i, carry):
        label = labels[i]
        parts = [rough[a, i] for a in range(4)]
        scale = 1.0 / (3.0 + (parts[0] + parts[1] + parts[2] + parts[3]))
        for a in range(3):
            own[i, a] = (jnp.where(label == a, 3.0, 0.0) + parts[a]) * scale
        for k in range(2):
            own[i, 3 + k] = pot[k, i]
        return carry

    lax.fori_loop(0, block, begin, 0)

    @pl.when(p == peers - 1)
    def _():
        def melt(j, carry):
            chosen = melt_index[j // SHIFT, lax.rem(j, SHIFT)]
            zero = jnp.zeros((rows, cols), jnp.float32)
            for a in range(3):
                state[j, a, pl.ds(low, rows)] = zero
            for k in range(2):
                value = zero + table[0, k]
                for e in range(1, table.shape[0]):
                    value = jnp.where(chosen == e, table[e, k], value)
                state[j, 3 + k, pl.ds(low, rows)] = value
            return carry

        lax.fori_loop(0, ROUNDS * SHIFT, melt, 0)

        def beyond(j, carry):
            for f in range(FIELDS):
                state[j, f, pl.ds(low, rows)] = jnp.zeros((rows, cols), jnp.float32)
            return carry

        lax.fori_loop(ROUNDS * SHIFT, stream, beyond, 0)

    pl.semaphore_wait(barrier, jnp.where(p > 0, 3, 2))

    def landed(j):
        return state.at[j, :, pl.ds(low, rows)]

    def first_copy(i):
        return pltpu.make_async_remote_copy(
            own.at[i], landed(i), z_send.at[i], z_recv.at[i],
            device_id=(below, q), device_id_type=MESH,
        )

    def pass_copy(j):
        return pltpu.make_async_remote_copy(
            landed(j), landed(block + j), z_send.at[block + j], z_recv.at[block + j],
            device_id=(below, q), device_id_type=MESH,
        )

    def side_copies(j):
        return (
            pltpu.make_async_remote_copy(
                state.at[j, :, pl.ds(low, halo)],
                state.at[j, :, pl.ds(high, halo)],
                x_send.at[0, j], x_recv.at[0, j],
                device_id=(p, left), device_id_type=MESH,
            ),
            pltpu.make_async_remote_copy(
                state.at[j, :, pl.ds(high - halo, halo)],
                state.at[j, :, pl.ds(PAD, halo)],
                x_send.at[1, j], x_recv.at[1, j],
                device_id=(p, right), device_id_type=MESH,
            ),
        )

    @pl.when(p > 0)
    def _():
        def send(i, carry):
            first_copy(i).start()
            return carry

        lax.fori_loop(0, block, send, 0)

    def arrive(j):
        @pl.when(p < peers - 1)
        def _():
            first_like = pltpu.make_async_remote_copy(
                landed(j), landed(j), z_send.at[j], z_recv.at[j],
                device_id=(below, q), device_id_type=MESH,
            )
            first_like.wait_recv()

        @pl.when((p > 0) & (j < stream - block))
        def _():
            pass_copy(j).start()

        for copy in side_copies(j):
            copy.start()

    gr = [[DT * grad[a, i] for i in range(3)] for a in range(4)]
    mid = [DT - 2.0 * (gr[a][0] + gr[a][1] + gr[a][2]) for a in range(4)]
    mid = [mid[a] + 1.0 for a in range(4)]
    cm = [0.25 * (comp[0, k] + comp[1, k] + comp[2, k] + comp[3, k]) for k in range(2)]
    beta = [[DT * (cm[k] - comp[a, k]) for k in range(2)] for a in range(3)]
    lm = 0.25 * (latent[0] + latent[1] + latent[2] + latent[3])
    gl = [DT * (lm - latent[a]) for a in range(3)]
    kd = [DT * diff[k] for k in range(2)]
    km = [1.0 - 6.0 * kd[k] for k in range(2)]
    rel = [[comp[a, k] - comp[3, k] for k in range(2)] for a in range(3)]
    flat3 = 2.0 * (gr[3][0] + gr[3][1] + gr[3][2]) + mid[3]

    def plane_step(s, j, source, target, edge):
        m = p * block + block + j
        turn = (s - 1) // STEPS
        top = planes - 1 + SHIFT * turn
        bottom = SHIFT * turn
        cen = j
        up = jnp.where(m == top, j, j + 1)
        down = jnp.where(m == bottom, j, j - 1)
        theta = (m.astype(jnp.float32) - 0.5 * planes) * (1.0 / planes)
        shift = [gl[a] * theta - 0.25 * flat3 + 0.25 for a in range(3)]

        def tile(at):
            here = pl.ds(at, HIGH)
            ctr, gs, xs, ys = [], [], [], []
            for f in range(FIELDS):
                c = source[cen, f, here]
                ctr.append(c)
                gs.append(source[up, f, here] + source[down, f, here])
                xs.append(source[cen, f, pl.ds(at - 1, HIGH)] + source[cen, f, pl.ds(at + 1, HIGH)])
                ys.append(pltpu.roll(c, 1, 1) + pltpu.roll(c, cols - 1, 1))
            w = [
                gr[a][0] * gs[a] + gr[a][1] * xs[a] + gr[a][2] * ys[a] + mid[a] * ctr[a]
                for a in range(3)
            ]
            w3 = (
                gr[3][0] * (gs[0] + gs[1] + gs[2])
                + gr[3][1] * (xs[0] + xs[1] + xs[2])
                + gr[3][2] * (ys[0] + ys[1] + ys[2])
                + mid[3] * (ctr[0] + ctr[1] + ctr[2])
            )
            mean = 0.25 * ((w[0] + w[1]) + (w[2] - w3))
            trial = [
                w[a] - mean + beta[a][0] * ctr[3] + beta[a][1] * ctr[4] + shift[a] for a in range(3)
            ]
            trial.append(1.0 - (trial[0] + trial[1] + trial[2]))
            clipped = [jnp.minimum(jnp.maximum(v, 0.0), 1.0) for v in trial]
            total = (clipped[0] + clipped[1]) + (clipped[2] + clipped[3])
            inv = pl.reciprocal(total, approx=True)
            inv = inv * (2.0 - total * inv)
            fresh = [clipped[a] * inv for a in range(3)]
            change = [fresh[a] - ctr[a] for a in range(3)]
            for k in range(2):
                around = (gs[3 + k] + xs[3 + k]) + ys[3 + k]
                value = km[k] * ctr[3 + k] + kd[k] * around
                fresh.append(value - (
                    rel[0][k] * change[0] + rel[1][k] * change[1] + rel[2][k] * change[2]
                ))
            put(at, HIGH, fresh)

        def put(at, size, fresh):
            if target is None:
                i = j - TOTAL
                out = pl.ds(at - low, size)
                for a in range(3):
                    phases[a, i, out] = fresh[a]
                phases[3, i, out] = 1.0 - (fresh[0] + fresh[1] + fresh[2])
                for k in range(2):
                    potentials[k, i, out] = fresh[3 + k]
            else:
                for f in range(FIELDS):
                    target[j, f, pl.ds(at, size)] = fresh[f]

        @pl.when(m <= top)
        def _():
            for at in range(PAD + 8 * edge, PAD + 2 * halo + rows - 8 * edge, HIGH):
                tile(at)

        @pl.when(m > top)
        def _():
            size = 2 * halo + rows - 16 * edge
            put(PAD + 8 * edge, size, [source[cen, f, pl.ds(PAD + 8 * edge, size)] for f in range(FIELDS)])

    for j in range(AHEAD):
        arrive(j)

    def diagonal(d, carry):
        @pl.when(d + AHEAD < stream)
        def _():
            arrive(d + AHEAD)

        for copy in side_copies(d):
            copy.wait_recv()

        @pl.when(d >= 2)
        def _():
            plane_step(1, d - 1, state, odd, 0)

        def pair(edge):
            def run(h, c):
                @pl.when(4 * h <= d)
                def _():
                    plane_step(2 * h, d - 2 * h, odd, even, edge)

                @pl.when(4 * h + 2 <= d)
                def _():
                    plane_step(2 * h + 1, d - 2 * h - 1, even, odd, edge)

                return c

            return run

        lax.fori_loop(1, 4, pair(0), 0)
        lax.fori_loop(4, 8, pair(1), 0)

        @pl.when(d >= 2 * TOTAL)
        def _():
            plane_step(TOTAL, d - TOTAL, odd, None, 2)

        return carry

    lax.fori_loop(0, stream, diagonal, 0)

    def settle(j, carry):
        for copy in side_copies(j):
            copy.wait_send()
        return carry

    lax.fori_loop(0, stream, settle, 0)

    @pl.when(p > 0)
    def _():
        def sent_own(i, carry):
            first_copy(i).wait_send()
            return carry

        lax.fori_loop(0, block, sent_own, 0)

        def sent_on(j, carry):
            pass_copy(j).wait_send()
            return carry

        lax.fori_loop(0, stream - block, sent_on, 0)


def solution(mesh):
    peers, lats = mesh.shape["grow"], mesh.shape["lat"]

    def on_device(labels, rough, pot, grad, comp, latent, diff, table, melt_index):
        block, rows, cols = labels.shape
        stream = block + 2 * TOTAL
        vmem = pl.BlockSpec(memory_space=pltpu.VMEM)
        smem = pl.BlockSpec(memory_space=pltpu.SMEM)
        return pl.pallas_call(
            functools.partial(kernel, peers, lats),
            out_shape=(
                jax.ShapeDtypeStruct((4, block, rows, cols), jnp.float32),
                jax.ShapeDtypeStruct((2, block, rows, cols), jnp.float32),
            ),
            in_specs=[vmem] * 4 + [smem] * 5,
            out_specs=(vmem, vmem),
            scratch_shapes=[
                pltpu.VMEM((block, FIELDS, rows, cols), jnp.float32),
                pltpu.VMEM((stream, FIELDS, rows + 2 * TOTAL + 2 * PAD, cols), jnp.float32),
pltpu.VMEM((stream, FIELDS, rows + 2 * TOTAL + 2 * PAD, cols), jnp.float32),
pltpu.VMEM((stream, FIELDS, rows + 2 * TOTAL + 2 * PAD, cols), jnp.float32),

                pltpu.SemaphoreType.DMA((stream,)),
                pltpu.SemaphoreType.DMA((stream,)),
                pltpu.SemaphoreType.DMA((2, stream)),
                pltpu.SemaphoreType.DMA((2, stream)),
            ],
            compiler_params=pltpu.CompilerParams(
                collective_id=0, has_side_effects=True, vmem_limit_bytes=48 << 20
            ),
        )(labels, rough, pot, melt_index, grad, comp, latent, diff, table)

    placed = (
        P("grow", "lat", None),
        P(None, "grow", "lat", None),
        P(None, "grow", "lat", None),
        P(),
        P(),
        P(),
        P(),
        P(),
        P(None, None, "lat", None),
    )
    return jax.shard_map(
        on_device,
        mesh=mesh,
        in_specs=placed,
        out_specs=(P(None, "grow", "lat", None), P(None, "grow", "lat", None)),
        check_vma=False,
    )
```

time: 487 us -> 215 us (0.44); the launches traced: 480 us -> 215 us
  Pallas kernels: 0 us -> 207 us
  other arithmetic: 160 us -> 0 us
  starting transfers between devices: 145 us -> 0 us
  waiting for transfers between devices: 127 us -> 0 us
  local copies, waits for them, and re-layouts: 39.9 us -> 7.47 us
  loops' own time: 4.98 us -> 0 us
    pallas_call x0 -> x1, Pallas kernels: none -> 207 us  [on_device(): pl.pallas_call(functools.partial(kernel, peers, lats), out_shape=(jax.Sha...]
    ppermute x68 -> x0, starting transfers between devices: 145 us -> none  [the longest x32 111 us: padded_2(): lax.ppermute(last, axis, up)]
    ppermute x68 -> x0, waiting for transfers between devices: 127 us -> none  [the longest x4 82.2 us: passed_along(): return lax.ppermute(block, axis, route)]
    sub x48 -> x0, other arithmetic: 86.6 us -> none  [the longest x16 34.8 us: advance(): rhs = lap_phi - 1.0 * (summed[None] - fracs) - psi]
    reduce_sum x25 -> x0, other arithmetic: 37.7 us -> none  [the longest x12 23.4 us: advance(): jnp.sum(composition[:, 0][:, None, None, None] * change, axis=0)]
    slice x62 -> x0, local copies, waits for them, and re-layouts: 35 us -> none  [the longest x32 23.1 us: advance(): ysum = jnp.roll(center, 1, 3) + jnp.roll(center, -1, 3) - 2.0 * center]
    select_n x20 -> x0, other arithmetic: 12.4 us -> none  [the longest x16 10 us: settle(): return jnp.where((place == final) & (rows >= margin + block), upper, out)]
    div x25 -> x0, other arithmetic: 12 us -> none  [the longest x4 9.43 us: advance(): newphi = clipped / jnp.sum(clipped, axis=0)[None]]
  transfers between devices with their start and end apart: 68 -> 0, of which waited for: 22 -> 0; matrix products, arithmetic and copies ran while one was open for 2% -> 0% of each run, Pallas kernels for 0% -> 0%
where the time goes in v1:
time: 215 us
  Pallas kernels  207 us (96%)
  local copies, waits for them, and re-layouts  7.47 us (3%)
    pallas_call x1, Pallas kernels, on_device(): pl.pallas_call(functools.partial(kernel, peers, lats), out_shape=(jax.Sha...  207 us
    unnamed x20, local copies, waits for them, and re-layouts  7.47 us

profile of v1, /device:TPU:249, one launch (start us, length us, event | category | flops | bytes accessed | tf_op | source)
XLA Modules:
  0.0 214.7 jit_solution(15172021111426434715)
XLA Ops:
  0.6 0.0 copy-start.7
  0.6 0.8 copy.11.comp
  1.4 0.0 copy-done.7
  1.4 0.0 copy-start.4
  1.4 0.0 copy-start.5
  1.4 0.0 copy-start.6
  1.4 0.1 copy.12.table
  1.5 0.6 copy-done.4
  2.1 0.0 copy-done.5
  2.1 0.0 copy-done.6
  2.1 0.0 copy-start
  2.1 1.2 copy-done
  3.3 0.0 copy-start.1
  3.3 1.0 copy-done.1
  4.4 0.0 copy-start.2
  4.4 1.0 copy-done.2
  5.4 0.0 copy-start.3
  5.4 0.9 copy-done.3
  6.4 206.6 %shard_map.104 = (f32[4,16,32,128]{3,2,1,0:T(8,128)S(1)}, f32[2,16,32,128]{3,2,1,0:T(8,128)S(1)}) custom-call(s32[16,32,128]{2,1,0:T(8,128)S(1)} %copy-done.3, f32[4,16,32,128]{3,2,1,0:T(8,128)S(1)} %copy-done, f32[2,16,32,128]{3,2,1,0:T(8,128)S(1)} %copy-done.1, s32[4,8,32,128]{3,2,1,0:T(8,128)S(1)} %copy-done.2, f32[4,3]{1,0:T(4,128)S(1)} %copy-done.4, ...), custom_call_target="tpu_custom_call" | custom-call | tf_op jit(solution)/shard_map/pallas_call | solution.py:312
  213.0 1.0 copy.15
  214.0 0.8 copy.16
Async XLA Ops:
  0.6 0.8 copy-start.7
  1.4 0.7 copy-start.4
  1.4 0.7 copy-start.5
  1.4 0.7 copy-start.6
  2.1 1.2 copy-start
  3.3 1.0 copy-start.1
  4.4 1.0 copy-start.2
  5.4 0.9 copy-start.3

commit v2 on v1

v2 whole, which is shorter than its diff:
```python
import functools

import jax
import jax.numpy as jnp
from jax import lax
from jax.experimental import pallas as pl
from jax.experimental.pallas import tpu as pltpu
from jax.sharding import PartitionSpec as P

MESH = pl.DeviceIdType.MESH
STEPS = 4
ROUNDS = 4
SHIFT = 8
DT = 0.04
TOTAL = STEPS * ROUNDS
FIELDS = 5
PAD = 8
LEAD = 3
LINE = 8
GROUP = 3
GROUPS = 5
HIGH = 16


def kernel(
    peers,
    lats,
    labels,
    rough,
    pot,
    melt_index,
    grad,
    comp,
    latent,
    diff,
    table,
    phases,
    potentials,
    odd,
    even,
    z_send,
    z_recv,
    x_send,
    x_recv,
    own_send,
    own_recv,
    detour,
    d_send,
    d_recv,
):
    block, rows, cols = labels.shape
    halo = TOTAL
    low = PAD + halo
    high = low + rows
    planes = peers * block
    p = lax.axis_index("grow")
    q = lax.axis_index("lat")
    below = jnp.maximum(p - 1, 0)
    above = jnp.minimum(p + 1, peers - 1)
    z = lax.rem(p, LINE)
    turns = (z == 0) & (p >= LINE)
    helps = (z == 0) & (p < peers - LINE)
    left = lax.rem(q + lats - 1, lats)
    right = lax.rem(q + 1, lats)

    barrier = pltpu.get_barrier_semaphore()
    for side in (left, right):
        pl.semaphore_signal(barrier, inc=1, device_id=(p, side), device_id_type=MESH)

    @pl.when(p < peers - 1)
    def _():
        pl.semaphore_signal(barrier, inc=1, device_id=(above, q), device_id_type=MESH)

    @pl.when(helps)
    def _():
        pl.semaphore_signal(
            barrier, inc=1, device_id=(jnp.minimum(p + LINE, peers - 1), q), device_id_type=MESH
        )

    @pl.when((z == LINE - 1) & (p < peers - 1))
    def _():
        pl.semaphore_signal(
            barrier, inc=1, device_id=(jnp.maximum(p - LINE + 1, 0), q), device_id_type=MESH
        )

    def begin(i, carry):
        label = labels[i]
        parts = [rough[a, i] for a in range(4)]
        scale = 1.0 / (3.0 + (parts[0] + parts[1] + parts[2] + parts[3]))
        for a in range(3):
            even[i, a, pl.ds(low, rows)] = (jnp.where(label == a, 3.0, 0.0) + parts[a]) * scale
        for k in range(2):
            even[i, 3 + k, pl.ds(low, rows)] = pot[k, i]
        return carry

    lax.fori_loop(0, block, begin, 0)
    pl.semaphore_wait(
        barrier,
        2 + (p > 0).astype(jnp.int32) + turns.astype(jnp.int32) + helps.astype(jnp.int32),
    )

    def down_copies(t, field):
        return [
            pltpu.make_async_remote_copy(
                field.at[2 * t + l, :, pl.ds(low, rows)],
                field.at[2 * t + block + l, :, pl.ds(low, rows)],
                z_send.at[t, l],
                z_recv.at[t, l],
                device_id=(below, q),
                device_id_type=MESH,
            )
            for l in range(LEAD)
        ]

    def turn_copies(k):
        return [
            pltpu.make_async_remote_copy(
                odd.at[4 * k + 2 + l, :, pl.ds(low, rows)],
                detour.at[k, l],
                z_send.at[2 * k + 1, l],
                d_recv.at[k, l],
                device_id=(jnp.maximum(p - LINE, 0), q),
                device_id_type=MESH,
            )
            for l in range(LEAD)
        ]

    def help_copies(k):
        return [
            pltpu.make_async_remote_copy(
                detour.at[k, l],
                odd.at[4 * k + 2 + block + l, :, pl.ds(low, rows)],
                d_send.at[k, l],
                z_recv.at[2 * k + 1, l],
                device_id=(jnp.minimum(p + LINE - 1, peers - 1), q),
                device_id_type=MESH,
            )
            for l in range(LEAD)
        ]

    def halo_copies(field, at, count, width, send, recv):
        return (
            pltpu.make_async_remote_copy(
                field.at[pl.ds(at, count), :, pl.ds(low, width)],
                field.at[pl.ds(at, count), :, pl.ds(high, width)],
                send.at[0], recv.at[0],
                device_id=(p, left), device_id_type=MESH,
            ),
            pltpu.make_async_remote_copy(
                field.at[pl.ds(at, count), :, pl.ds(high - width, width)],
                field.at[pl.ds(at, count), :, pl.ds(low - width, width)],
                send.at[1], recv.at[1],
                device_id=(p, right), device_id_type=MESH,
            ),
        )

    def own_copies(c):
        return halo_copies(even, 4 * c, 4, halo, own_send.at[c], own_recv.at[c])

    def side_copies(t, field, width):
        return halo_copies(field, 2 * t + block, LEAD, width, x_send.at[t], x_recv.at[t])

    def by_level(t, use):
        for parity, field in ((0, even), (1, odd)):
            for first, width in ((0, 16), (8, 8)):
                @pl.when((lax.rem(t, 2) == parity) & (t >= first) & (t < first + 8))
                def _():
                    use(field, width)

    for c in range(2):
        for copy in own_copies(c):
            copy.start()

    @pl.when(p > 0)
    def _():
        for copy in down_copies(0, even):
            copy.start()

    for c in range(2, 4):
        for copy in own_copies(c):
            copy.start()

    def melt(t, field):
        for l in range(LEAD):
            j = jnp.minimum(2 * t + l, ROUNDS * SHIFT - 1)
            chosen = melt_index[j // SHIFT, lax.rem(j, SHIFT)]
            zero = jnp.zeros((rows, cols), jnp.float32)
            for a in range(3):
                field[2 * t + block + l, a, pl.ds(low, rows)] = zero
            for k in range(2):
                value = zero + table[0, k]
                for e in range(1, table.shape[0]):
                    value = jnp.where(chosen == e, table[e, k], value)
                field[2 * t + block + l, 3 + k, pl.ds(low, rows)] = value

    def arrive(t):
        @pl.when(p < peers - 1)
        def _():
            for copy in down_copies(t, even):
                copy.wait_recv()

        @pl.when((p == peers - 1) & (lax.rem(t, 2) == 0))
        def _():
            melt(t, even)

        @pl.when((p == peers - 1) & (lax.rem(t, 2) == 1))
        def _():
            melt(t, odd)

        def go(field, width):
            for copy in side_copies(t, field, width):
                copy.start()

        by_level(t, go)

    def sides_done(t):
        def go(field, width):
            for copy in side_copies(t, field, width):
                copy.wait()

        by_level(t, go)

    gr = [[DT * grad[a, i] for i in range(3)] for a in range(4)]
    mid = [DT - 2.0 * (gr[a][0] + gr[a][1] + gr[a][2]) for a in range(4)]
    mid = [mid[a] + 1.0 for a in range(4)]
    cm = [0.25 * (comp[0, k] + comp[1, k] + comp[2, k] + comp[3, k]) for k in range(2)]
    beta = [[DT * (cm[k] - comp[a, k]) for k in range(2)] for a in range(3)]
    lm = 0.25 * (latent[0] + latent[1] + latent[2] + latent[3])
    gl = [DT * (lm - latent[a]) for a in range(3)]
    kd = [DT * diff[k] for k in range(2)]
    km = [1.0 - 6.0 * kd[k] for k in range(2)]
    rel = [[comp[a, k] - comp[3, k] for k in range(2)] for a in range(3)]
    flat3 = 2.0 * (gr[3][0] + gr[3][1] + gr[3][2]) + mid[3]

    def plane_step(s, j, source, target, edge):
        m = p * block + j
        turn = (s - 1) // STEPS
        top = planes - 1 + SHIFT * turn
        bottom = SHIFT * turn
        cen = j
        up = jnp.where(m == top, j, j + 1)
        down = jnp.where(m == bottom, j, j - 1)
        theta = (m.astype(jnp.float32) - 0.5 * planes) * (1.0 / planes)
        shift = [gl[a] * theta - 0.25 * flat3 + 0.25 for a in range(3)]

        def tile(at):
            here = pl.ds(at, HIGH)
            ctr, gs, xs, ys = [], [], [], []
            for f in range(FIELDS):
                c = source[cen, f, here]
                ctr.append(c)
                gs.append(source[up, f, here] + source[down, f, here])
                xs.append(source[cen, f, pl.ds(at - 1, HIGH)] + source[cen, f, pl.ds(at + 1, HIGH)])
                ys.append(pltpu.roll(c, 1, 1) + pltpu.roll(c, cols - 1, 1))
            w = [
                gr[a][0] * gs[a] + gr[a][1] * xs[a] + gr[a][2] * ys[a] + mid[a] * ctr[a]
                for a in range(3)
            ]
            w3 = (
                gr[3][0] * (gs[0] + gs[1] + gs[2])
                + gr[3][1] * (xs[0] + xs[1] + xs[2])
                + gr[3][2] * (ys[0] + ys[1] + ys[2])
                + mid[3] * (ctr[0] + ctr[1] + ctr[2])
            )
            mean = 0.25 * ((w[0] + w[1]) + (w[2] - w3))
            trial = [
                w[a] - mean + beta[a][0] * ctr[3] + beta[a][1] * ctr[4] + shift[a] for a in range(3)
            ]
            trial.append(1.0 - (trial[0] + trial[1] + trial[2]))
            clipped = [jnp.minimum(jnp.maximum(v, 0.0), 1.0) for v in trial]
            total = (clipped[0] + clipped[1]) + (clipped[2] + clipped[3])
            inv = pl.reciprocal(total, approx=True)
            inv = inv * (2.0 - total * inv)
            fresh = [clipped[a] * inv for a in range(3)]
            change = [fresh[a] - ctr[a] for a in range(3)]
            for k in range(2):
                around = (gs[3 + k] + xs[3 + k]) + ys[3 + k]
                value = km[k] * ctr[3 + k] + kd[k] * around
                fresh.append(value - (
                    rel[0][k] * change[0] + rel[1][k] * change[1] + rel[2][k] * change[2]
                ))
            put(at, HIGH, fresh)

        def put(at, size, fresh):
            if target is None:
                i = j - 2 * TOTAL
                out = pl.ds(at - low, size)
                for a in range(3):
                    phases[a, i, out] = fresh[a]
                phases[3, i, out] = 1.0 - (fresh[0] + fresh[1] + fresh[2])
                for k in range(2):
                    potentials[k, i, out] = fresh[3 + k]
            else:
                for f in range(FIELDS):
                    target[j, f, pl.ds(at, size)] = fresh[f]

        @pl.when(m <= top)
        def _():
            for at in range(PAD + 8 * edge, PAD + 2 * halo + rows - 8 * edge, HIGH):
                tile(at)

        @pl.when(m > top)
        def _():
            size = 2 * halo + rows - 16 * edge
            put(PAD + 8 * edge, size, [source[cen, f, pl.ds(PAD + 8 * edge, size)] for f in range(FIELDS)])

    def group(g, level):
        first = 2 * level + GROUP * g
        last = first + GROUP + jnp.where(g == GROUPS - 1, block - GROUP * GROUPS, 0)

        def run(source, target, edge):
            def one(j, c):
                plane_step(level, j, source, target, edge)
                return c

            lax.fori_loop(first, last, one, 0)

        for parity, source, target in ((1, even, odd), (0, odd, even)):
            for edge in range(2):
                @pl.when((lax.rem(level, 2) == parity) & (level // 8 == edge))
                def _():
                    run(source, target, edge)

        @pl.when(level == TOTAL)
        def _():
            run(odd, None, 2)

    def iteration(n, carry):
        @pl.when((n >= GROUPS - 1) & (n - GROUPS + 1 < TOTAL))
        def _():
            arrive(n - GROUPS + 1)

        def descend(k, c):
            g = GROUPS - 1 - k
            level = n - g

            @pl.when((g == GROUPS - 1) & (level >= 1))
            def _():
                sides_done(level - 1)

            @pl.when(level == 1)
            def _():
                for c in range(4):
                    @pl.when(g == max(c - 1, 0))
                    def _():
                        for copy in own_copies(c):
                            copy.wait()

            @pl.when((level >= 1) & (level <= TOTAL))
            def _():
                group(g, level)

            return c

        lax.fori_loop(0, GROUPS, descend, 0)

        @pl.when(helps & (n >= 3) & (n - 2 < TOTAL) & (lax.rem(n, 2) == 1))
        def _():
            for copy in turn_copies((n - 2) // 2):
                copy.wait_recv()
            for copy in help_copies((n - 2) // 2):
                copy.start()

        @pl.when((p > 0) & (n < TOTAL) & (lax.rem(n, 2) == 0))
        def _():
            for copy in down_copies(n, even):
                copy.start()

        @pl.when((p > 0) & (z > 0) & (n < TOTAL) & (lax.rem(n, 2) == 1))
        def _():
            for copy in down_copies(n, odd):
                copy.start()

        @pl.when(turns & (n < TOTAL) & (lax.rem(n, 2) == 1))
        def _():
            for copy in turn_copies(n // 2):
                copy.start()

        return carry

    lax.fori_loop(1, TOTAL + GROUPS, iteration, 0)

    @pl.when(p > 0)
    def _():
        def sent(t, carry):
            for copy in down_copies(t, even):
                copy.wait_send()
            return carry

        lax.fori_loop(0, TOTAL, sent, 0)

    @pl.when(helps)
    def _():
        def helped(k, carry):
            for copy in help_copies(k):
                copy.wait_send()
            return carry

        lax.fori_loop(0, TOTAL // 2, helped, 0)


def solution(mesh):
    peers, lats = mesh.shape["grow"], mesh.shape["lat"]

    def on_device(labels, rough, pot, grad, comp, latent, diff, table, melt_index):
        block, rows, cols = labels.shape
        span = block + 2 * TOTAL + LEAD
        field = pltpu.VMEM((span, FIELDS, rows + 2 * TOTAL + 2 * PAD, cols), jnp.float32)
        vmem = pl.BlockSpec(memory_space=pltpu.VMEM)
        smem = pl.BlockSpec(memory_space=pltpu.SMEM)
        return pl.pallas_call(
            functools.partial(kernel, peers, lats),
            out_shape=(
                jax.ShapeDtypeStruct((4, block, rows, cols), jnp.float32),
                jax.ShapeDtypeStruct((2, block, rows, cols), jnp.float32),
            ),
            in_specs=[vmem] * 4 + [smem] * 5,
            out_specs=(vmem, vmem),
            scratch_shapes=[field, field] + [
                pltpu.SemaphoreType.DMA((TOTAL, LEAD)),
                pltpu.SemaphoreType.DMA((TOTAL, LEAD)),
                pltpu.SemaphoreType.DMA((TOTAL, 2)),
                pltpu.SemaphoreType.DMA((TOTAL, 2)),
                pltpu.SemaphoreType.DMA((4, 2)),
                pltpu.SemaphoreType.DMA((4, 2)),
                pltpu.VMEM((TOTAL // 2, LEAD, FIELDS, rows, cols), jnp.float32),
                pltpu.SemaphoreType.DMA((TOTAL // 2, LEAD)),
                pltpu.SemaphoreType.DMA((TOTAL // 2, LEAD)),
            ],
            compiler_params=pltpu.CompilerParams(
                collective_id=0, has_side_effects=True, vmem_limit_bytes=48 << 20
            ),
        )(labels, rough, pot, melt_index, grad, comp, latent, diff, table)

    placed = (
        P("grow", "lat", None),
        P(None, "grow", "lat", None),
        P(None, "grow", "lat", None),
        P(),
        P(),
        P(),
        P(),
        P(),
        P(None, None, "lat", None),
    )
    return jax.shard_map(
        on_device,
        mesh=mesh,
        in_specs=placed,
        out_specs=(P(None, "grow", "lat", None), P(None, "grow", "lat", None)),
        check_vma=False,
    )
```

time: 215 us -> 137 us (0.64)
  Pallas kernels: 207 us -> 129 us
    pallas_call x1, Pallas kernels: 207 us -> 129 us  [on_device(): pl.pallas_call(functools.partial(kernel, peers, lats), out_shape=(jax.Sha...]
where the time goes in v2:
time: 137 us
  Pallas kernels  129 us (94%)
  local copies, waits for them, and re-layouts  7.47 us (5%)
    pallas_call x1, Pallas kernels, on_device(): pl.pallas_call(functools.partial(kernel, peers, lats), out_shape=(jax.Sha...  129 us
    unnamed x20, local copies, waits for them, and re-layouts  7.47 us

profile of v2, /device:TPU:249, one launch (start us, length us, event | category | flops | bytes accessed | tf_op | source)
XLA Modules:
  0.0 136.8 jit_solution(15750195572851302111)
XLA Ops:
  0.6 0.0 copy-start.7
  0.6 0.8 copy.11.comp
  1.4 0.0 copy-done.7
  1.4 0.0 copy-start.4
  1.4 0.0 copy-start.5
  1.4 0.0 copy-start.6
  1.4 0.1 copy.12.table
  1.5 0.6 copy-done.4
  2.1 0.0 copy-done.5
  2.1 0.0 copy-done.6
  2.1 0.0 copy-start
  2.1 1.2 copy-done
  3.3 0.0 copy-start.1
  3.3 1.0 copy-done.1
  4.4 0.0 copy-start.2
  4.4 1.0 copy-done.2
  5.4 0.0 copy-start.3
  5.4 0.9 copy-done.3
  6.4 128.7 %shard_map.104 = (f32[4,16,32,128]{3,2,1,0:T(8,128)S(1)}, f32[2,16,32,128]{3,2,1,0:T(8,128)S(1)}) custom-call(s32[16,32,128]{2,1,0:T(8,128)S(1)} %copy-done.3, f32[4,16,32,128]{3,2,1,0:T(8,128)S(1)} %copy-done, f32[2,16,32,128]{3,2,1,0:T(8,128)S(1)} %copy-done.1, s32[4,8,32,128]{3,2,1,0:T(8,128)S(1)} %copy-done.2, f32[4,3]{1,0:T(4,128)S(1)} %copy-done.4, ...), custom_call_target="tpu_custom_call" | custom-call | tf_op jit(solution)/shard_map/pallas_call | solution.py:411
  135.1 1.0 copy.15
  136.1 0.8 copy.16
Async XLA Ops:
  0.6 0.8 copy-start.7
  1.4 0.7 copy-start.4
  1.4 0.7 copy-start.5
  1.4 0.7 copy-start.6
  2.1 1.2 copy-start
  3.3 1.0 copy-start.1
  4.4 1.0 copy-start.2
  5.4 0.9 copy-start.3

commit v3 on v2

--- a/solution.py
+++ b/solution.py
@@ -17,6 +17,8 @@
 PAD = 8
 LEAD = 3
 LINE = 8
+HALO = 8
+HELP_AT = 2
 GROUP = 3
 GROUPS = 5
 HIGH = 16
@@ -25,10 +27,10 @@
 def kernel(
     peers,
     lats,
-    labels,
-    rough,
-    pot,
-    melt_index,
+    labels_in,
+    rough_in,
+    pot_in,
+    melt_in,
     grad,
     comp,
     latent,
@@ -47,9 +49,14 @@
     detour,
     d_send,
     d_recv,
+    labels,
+    rough,
+    pot,
+    melt_index,
+    load,
 ):
     block, rows, cols = labels.shape
-    halo = TOTAL
+    halo = HALO
     low = PAD + halo
     high = low + rows
     planes = peers * block
@@ -63,6 +70,19 @@
     left = lax.rem(q + lats - 1, lats)
     right = lax.rem(q + 1, lats)
 
+    def loads(c):
+        some = pl.ds(4 * c, 4)
+        return (
+            pltpu.make_async_copy(labels_in.at[some], labels.at[some], load.at[3 * c]),
+            pltpu.make_async_copy(rough_in.at[:, some], rough.at[:, some], load.at[3 * c + 1]),
+            pltpu.make_async_copy(pot_in.at[:, some], pot.at[:, some], load.at[3 * c + 2]),
+        )
+
+    melt_load = pltpu.make_async_copy(melt_in, melt_index, load.at[12])
+    for c in range(4):
+        for copy in loads(c):
+            copy.start()
+
     barrier = pltpu.get_barrier_semaphore()
     for side in (left, right):
         pl.semaphore_signal(barrier, inc=1, device_id=(p, side), device_id_type=MESH)
@@ -93,92 +113,100 @@
             even[i, 3 + k, pl.ds(low, rows)] = pot[k, i]
         return carry
 
-    lax.fori_loop(0, block, begin, 0)
+    def start_part(c):
+        for copy in loads(c):
+            copy.wait()
+        lax.fori_loop(4 * c, 4 * c + 4, begin, 0)
+
+    start_part(0)
     pl.semaphore_wait(
         barrier,
         2 + (p > 0).astype(jnp.int32) + turns.astype(jnp.int32) + helps.astype(jnp.int32),
     )
 
-    def down_copies(t, field):
-        return [
-            pltpu.make_async_remote_copy(
-                field.at[2 * t + l, :, pl.ds(low, rows)],
-                field.at[2 * t + block + l, :, pl.ds(low, rows)],
-                z_send.at[t, l],
-                z_recv.at[t, l],
-                device_id=(below, q),
-                device_id_type=MESH,
-            )
-            for l in range(LEAD)
-        ]
-
-    def turn_copies(k):
-        return [
-            pltpu.make_async_remote_copy(
-                odd.at[4 * k + 2 + l, :, pl.ds(low, rows)],
-                detour.at[k, l],
-                z_send.at[2 * k + 1, l],
-                d_recv.at[k, l],
-                device_id=(jnp.maximum(p - LINE, 0), q),
-                device_id_type=MESH,
-            )
-            for l in range(LEAD)
-        ]
-
-    def help_copies(k):
-        return [
-            pltpu.make_async_remote_copy(
-                detour.at[k, l],
-                odd.at[4 * k + 2 + block + l, :, pl.ds(low, rows)],
-                d_send.at[k, l],
-                z_recv.at[2 * k + 1, l],
-                device_id=(jnp.minimum(p + LINE - 1, peers - 1), q),
-                device_id_type=MESH,
-            )
-            for l in range(LEAD)
-        ]
-
-    def halo_copies(field, at, count, width, send, recv):
+    def lands(t, l, field):
+        return field.at[2 * t + block + l, :, pl.ds(low, rows)]
+
+    def down_copy(t, l, field):
+        return pltpu.make_async_remote_copy(
+            field.at[2 * t + l, :, pl.ds(low, rows)],
+            lands(t, l, field),
+            z_send.at[t, l],
+            z_recv.at[t, l],
+            device_id=(below, q),
+            device_id_type=MESH,
+        )
+
+    def turn_copy(t, l, field):
+        return pltpu.make_async_remote_copy(
+            field.at[2 * t + l, :, pl.ds(low, rows)],
+            detour.at[t, l],
+            z_send.at[t, l],
+            d_recv.at[t, l],
+            device_id=(jnp.maximum(p - LINE, 0), q),
+            device_id_type=MESH,
+        )
+
+    def help_copy(t, l, field):
+        return pltpu.make_async_remote_copy(
+            detour.at[t, l],
+            lands(t, l, field),
+            d_send.at[t, l],
+            z_recv.at[t, l],
+            device_id=(jnp.minimum(p + LINE - 1, peers - 1), q),
+            device_id_type=MESH,
+        )
+
+    def send_down(t, parity, field):
+        @pl.when(turns)
+        def _():
+            for l in range(LEAD):
+                (turn_copy if l <= parity else down_copy)(t, l, field).start()
+
+        @pl.when((p > 0) & (z > 0))
+        def _():
+            for l in range(LEAD):
+                down_copy(t, l, field).start()
+
+    def help_down(t, parity, field):
+        for l in range(parity + 1):
+            turn_copy(t, l, field).wait_recv()
+            help_copy(t, l, field).start()
+
+    def halo_copies(field, at, count, send, recv):
         return (
             pltpu.make_async_remote_copy(
-                field.at[pl.ds(at, count), :, pl.ds(low, width)],
-                field.at[pl.ds(at, count), :, pl.ds(high, width)],
+                field.at[pl.ds(at, count), :, pl.ds(low, halo)],
+                field.at[pl.ds(at, count), :, pl.ds(high, halo)],
                 send.at[0], recv.at[0],
                 device_id=(p, left), device_id_type=MESH,
             ),
             pltpu.make_async_remote_copy(
-                field.at[pl.ds(at, count), :, pl.ds(high - width, width)],
-                field.at[pl.ds(at, count), :, pl.ds(low - width, width)],
+                field.at[pl.ds(at, count), :, pl.ds(high - halo, halo)],
+                field.at[pl.ds(at, count), :, pl.ds(low - halo, halo)],
                 send.at[1], recv.at[1],
                 device_id=(p, right), device_id_type=MESH,
             ),
         )
 
     def own_copies(c):
-        return halo_copies(even, 4 * c, 4, halo, own_send.at[c], own_recv.at[c])
-
-    def side_copies(t, field, width):
-        return halo_copies(field, 2 * t + block, LEAD, width, x_send.at[t], x_recv.at[t])
-
-    def by_level(t, use):
-        for parity, field in ((0, even), (1, odd)):
-            for first, width in ((0, 16), (8, 8)):
-                @pl.when((lax.rem(t, 2) == parity) & (t >= first) & (t < first + 8))
-                def _():
-                    use(field, width)
-
-    for c in range(2):
+        return halo_copies(even, 4 * c, 4, own_send.at[c], own_recv.at[c])
+
+    def side_copies(t, field):
+        return halo_copies(field, 2 * t + block, LEAD, x_send.at[t], x_recv.at[t])
+
+    send_down(0, 0, even)
+
+    for c in range(4):
+        if c > 0:
+            start_part(c)
         for copy in own_copies(c):
             copy.start()
 
-    @pl.when(p > 0)
-    def _():
-        for copy in down_copies(0, even):
-            copy.start()
-
-    for c in range(2, 4):
-        for copy in own_copies(c):
-            copy.start()
+    @pl.when(p == peers - 1)
+    def _():
+        melt_load.start()
+        melt_load.wait()
 
     def melt(t, field):
         for l in range(LEAD):
@@ -188,48 +216,44 @@
             for a in range(3):
                 field[2 * t + block + l, a, pl.ds(low, rows)] = zero
             for k in range(2):
-                value = zero + table[0, k]
-                for e in range(1, table.shape[0]):
-                    value = jnp.where(chosen == e, table[e, k], value)
+                value = zero + table[k, 0]
+                for e in range(1, table.shape[1]):
+                    value = jnp.where(chosen == e, table[k, e], value)
                 field[2 * t + block + l, 3 + k, pl.ds(low, rows)] = value
 
     def arrive(t):
         @pl.when(p < peers - 1)
         def _():
-            for copy in down_copies(t, even):
-                copy.wait_recv()
-
-        @pl.when((p == peers - 1) & (lax.rem(t, 2) == 0))
-        def _():
-            melt(t, even)
-
-        @pl.when((p == peers - 1) & (lax.rem(t, 2) == 1))
-        def _():
-            melt(t, odd)
-
-        def go(field, width):
-            for copy in side_copies(t, field, width):
-                copy.start()
-
-        by_level(t, go)
+            for l in range(LEAD):
+                down_copy(t, l, even).wait_recv()
+
+        for parity, field in ((0, even), (1, odd)):
+            @pl.when((p == peers - 1) & (lax.rem(t, 2) == parity))
+            def _():
+                melt(t, field)
+
+            @pl.when(lax.rem(t, 2) == parity)
+            def _():
+                for copy in side_copies(t, field):
+                    copy.start()
 
     def sides_done(t):
-        def go(field, width):
-            for copy in side_copies(t, field, width):
-                copy.wait()
-
-        by_level(t, go)
+        for parity, field in ((0, even), (1, odd)):
+            @pl.when(lax.rem(t, 2) == parity)
+            def _():
+                for copy in side_copies(t, field):
+                    copy.wait()
 
     gr = [[DT * grad[a, i] for i in range(3)] for a in range(4)]
     mid = [DT - 2.0 * (gr[a][0] + gr[a][1] + gr[a][2]) for a in range(4)]
     mid = [mid[a] + 1.0 for a in range(4)]
-    cm = [0.25 * (comp[0, k] + comp[1, k] + comp[2, k] + comp[3, k]) for k in range(2)]
-    beta = [[DT * (cm[k] - comp[a, k]) for k in range(2)] for a in range(3)]
+    cm = [0.25 * (comp[k, 0] + comp[k, 1] + comp[k, 2] + comp[k, 3]) for k in range(2)]
+    beta = [[DT * (cm[k] - comp[k, a]) for k in range(2)] for a in range(3)]
     lm = 0.25 * (latent[0] + latent[1] + latent[2] + latent[3])
     gl = [DT * (lm - latent[a]) for a in range(3)]
     kd = [DT * diff[k] for k in range(2)]
     km = [1.0 - 6.0 * kd[k] for k in range(2)]
-    rel = [[comp[a, k] - comp[3, k] for k in range(2)] for a in range(3)]
+    rel = [[comp[k, a] - comp[k, 3] for k in range(2)] for a in range(3)]
     flat3 = 2.0 * (gr[3][0] + gr[3][1] + gr[3][2]) + mid[3]
 
     def plane_step(s, j, source, target, edge):
@@ -308,22 +332,24 @@
         first = 2 * level + GROUP * g
         last = first + GROUP + jnp.where(g == GROUPS - 1, block - GROUP * GROUPS, 0)
 
-        def run(source, target, edge):
+        lowest = first + jnp.where(g == 0, 2, 0)
+
+        def run(source, target, edge, begin, end):
             def one(j, c):
                 plane_step(level, j, source, target, edge)
                 return c
 
-            lax.fori_loop(first, last, one, 0)
+            lax.fori_loop(begin, end, one, 0)
 
         for parity, source, target in ((1, even, odd), (0, odd, even)):
-            for edge in range(2):
-                @pl.when((lax.rem(level, 2) == parity) & (level // 8 == edge))
-                def _():
-                    run(source, target, edge)
+            @pl.when((lax.rem(level, 2) == parity) & (level < TOTAL))
+            def _():
+                run(source, target, 1, first, lowest)
+                run(source, target, 0, lowest, last)
 
         @pl.when(level == TOTAL)
         def _():
-            run(odd, None, 2)
+            run(odd, None, 1, first, last)
 
     def iteration(n, carry):
         @pl.when((n >= GROUPS - 1) & (n - GROUPS + 1 < TOTAL))
@@ -350,31 +376,21 @@
             def _():
                 group(g, level)
 
+            for parity, field in ((0, even), (1, odd)):
+                @pl.when(
+                    helps & (k == HELP_AT) & (n >= 2) & (n - 2 < TOTAL) & (lax.rem(n, 2) == parity)
+                )
+                def _():
+                    help_down(n - 2, parity, field)
+
             return c
 
         lax.fori_loop(0, GROUPS, descend, 0)
 
-        @pl.when(helps & (n >= 3) & (n - 2 < TOTAL) & (lax.rem(n, 2) == 1))
-        def _():
-            for copy in turn_copies((n - 2) // 2):
-                copy.wait_recv()
-            for copy in help_copies((n - 2) // 2):
-                copy.start()
-
-        @pl.when((p > 0) & (n < TOTAL) & (lax.rem(n, 2) == 0))
-        def _():
-            for copy in down_copies(n, even):
-                copy.start()
-
-        @pl.when((p > 0) & (z > 0) & (n < TOTAL) & (lax.rem(n, 2) == 1))
-        def _():
-            for copy in down_copies(n, odd):
-                copy.start()
-
-        @pl.when(turns & (n < TOTAL) & (lax.rem(n, 2) == 1))
-        def _():
-            for copy in turn_copies(n // 2):
-                copy.start()
+        for parity, field in ((0, even), (1, odd)):
+            @pl.when((n < TOTAL) & (lax.rem(n, 2) == parity))
+            def _():
+                send_down(n, parity, field)
 
         return carry
 
@@ -383,17 +399,18 @@
     @pl.when(p > 0)
     def _():
         def sent(t, carry):
-            for copy in down_copies(t, even):
-                copy.wait_send()
+            for l in range(LEAD):
+                down_copy(t, l, even).wait_send()
             return carry
 
         lax.fori_loop(0, TOTAL, sent, 0)
 
     @pl.when(helps)
     def _():
-        def helped(k, carry):
-            for copy in help_copies(k):
-                copy.wait_send()
+        def helped(h, carry):
+            for parity, field in ((0, even), (1, odd)):
+                for l in range(parity + 1):
+                    help_copy(2 * h + parity, l, field).wait_send()
             return carry
 
         lax.fori_loop(0, TOTAL // 2, helped, 0)
@@ -405,8 +422,9 @@
     def on_device(labels, rough, pot, grad, comp, latent, diff, table, melt_index):
         block, rows, cols = labels.shape
         span = block + 2 * TOTAL + LEAD
-        field = pltpu.VMEM((span, FIELDS, rows + 2 * TOTAL + 2 * PAD, cols), jnp.float32)
+        field = pltpu.VMEM((span, FIELDS, rows + 2 * HALO + 2 * PAD, cols), jnp.float32)
         vmem = pl.BlockSpec(memory_space=pltpu.VMEM)
+        hbm = pl.BlockSpec(memory_space=pltpu.HBM)
         smem = pl.BlockSpec(memory_space=pltpu.SMEM)
         return pl.pallas_call(
             functools.partial(kernel, peers, lats),
@@ -414,7 +432,7 @@
                 jax.ShapeDtypeStruct((4, block, rows, cols), jnp.float32),
                 jax.ShapeDtypeStruct((2, block, rows, cols), jnp.float32),
             ),
-            in_specs=[vmem] * 4 + [smem] * 5,
+            in_specs=[hbm] * 4 + [smem] * 5,
             out_specs=(vmem, vmem),
             scratch_shapes=[field, field] + [
                 pltpu.SemaphoreType.DMA((TOTAL, LEAD)),
@@ -423,14 +441,19 @@
                 pltpu.SemaphoreType.DMA((TOTAL, 2)),
                 pltpu.SemaphoreType.DMA((4, 2)),
                 pltpu.SemaphoreType.DMA((4, 2)),
-                pltpu.VMEM((TOTAL // 2, LEAD, FIELDS, rows, cols), jnp.float32),
-                pltpu.SemaphoreType.DMA((TOTAL // 2, LEAD)),
-                pltpu.SemaphoreType.DMA((TOTAL // 2, LEAD)),
+                pltpu.VMEM((TOTAL, 2, FIELDS, rows, cols), jnp.float32),
+                pltpu.SemaphoreType.DMA((TOTAL, 2)),
+                pltpu.SemaphoreType.DMA((TOTAL, 2)),
+                pltpu.VMEM((block, rows, cols), jnp.int32),
+                pltpu.VMEM((4, block, rows, cols), jnp.float32),
+                pltpu.VMEM((2, block, rows, cols), jnp.float32),
+                pltpu.VMEM((ROUNDS, SHIFT, rows, cols), jnp.int32),
+                pltpu.SemaphoreType.DMA((13,)),
             ],
             compiler_params=pltpu.CompilerParams(
-                collective_id=0, has_side_effects=True, vmem_limit_bytes=48 << 20
+                collective_id=0, has_side_effects=True, vmem_limit_bytes=60 << 20
             ),
-        )(labels, rough, pot, melt_index, grad, comp, latent, diff, table)
+        )(labels, rough, pot, melt_index, grad, comp.T, latent, diff, table.T)
 
     placed = (
         P("grow", "lat", None),

time: 137 us -> 109 us (0.80); the launches traced: 137 us -> 107 us
  Pallas kernels: 129 us -> 103 us
  local copies, waits for them, and re-layouts: 7.47 us -> 3.12 us
    pallas_call x1, Pallas kernels: 129 us -> 103 us  [on_device(): pl.pallas_call(functools.partial(kernel, peers, lats), out_shape=(jax.Sha...]
    unnamed x20 -> x4, local copies, waits for them, and re-layouts: 7.47 us -> 3.12 us
where the time goes in v3:
time: 109 us; the launch traced here: 107 us
  Pallas kernels  103 us (94%)
  local copies, waits for them, and re-layouts  3.12 us (3%)
    pallas_call x1, Pallas kernels, on_device(): pl.pallas_call(functools.partial(kernel, peers, lats), out_shape=(jax.Sha...  103 us
    unnamed x4, local copies, waits for them, and re-layouts  3.12 us

profile of v3, /device:TPU:249, one launch (start us, length us, event | category | flops | bytes accessed | tf_op | source)
XLA Modules:
  0.0 107.0 jit_solution(2804407243495820506)
XLA Ops:
  0.6 103.2 %shard_map.104 = (f32[4,16,32,128]{3,2,1,0:T(8,128)}, f32[2,16,32,128]{3,2,1,0:T(8,128)}) custom-call(s32[16,32,128]{2,1,0:T(8,128)} %labels_in.1, f32[4,16,32,128]{3,2,1,0:T(8,128)} %rough_in.1, f32[2,16,32,128]{3,2,1,0:T(8,128)} %pot_in.1, s32[4,8,32,128]{3,2,1,0:T(8,128)} %melt_in.1, f32[4,3]{1,0:T(4,128)} %grad.1, f32[2,4]{1,0:T(2,128)} %bitcast.2, ...), custom_call_target="tpu_custom_call" | custom-call | tf_op jit(solution)/shard_map/pallas_call | solution.py:429
  103.9 0.0 copy-start
  103.9 2.3 %copy.13 = f32[4,16,32,128]{3,2,1,0:T(8,128)} copy(f32[4,16,32,128]{3,2,1,0:T(8,128)} %get-tuple-element.4) | data formatting | bytes 2097152
  106.2 0.0 copy-done
  106.2 0.8 copy.14
Async XLA Ops:
  103.9 2.3 %copy-start = (f32[2,16,32,128]{3,2,1,0:T(8,128)S(1)}, f32[2,16,32,128]{3,2,1,0:T(8,128)}, u32[]{:S(2)}) copy-start(f32[2,16,32,128]{3,2,1,0:T(8,128)} %get-tuple-element.5) | copy-start | bytes 1572868

commit v4 on v3

--- a/solution.py
+++ b/solution.py
@@ -18,7 +18,7 @@
 LEAD = 3
 LINE = 8
 HALO = 8
-HELP_AT = 2
+HELP_AT = 3
 GROUP = 3
 GROUPS = 5
 HIGH = 16
@@ -36,8 +36,8 @@
     latent,
     diff,
     table,
-    phases,
-    potentials,
+    phases_out,
+    potentials_out,
     odd,
     even,
     z_send,
@@ -54,6 +54,9 @@
     pot,
     melt_index,
     load,
+    phases,
+    potentials,
+    store,
 ):
     block, rows, cols = labels.shape
     halo = HALO
@@ -79,10 +82,6 @@
         )
 
     melt_load = pltpu.make_async_copy(melt_in, melt_index, load.at[12])
-    for c in range(4):
-        for copy in loads(c):
-            copy.start()
-
     barrier = pltpu.get_barrier_semaphore()
     for side in (left, right):
         pl.semaphore_signal(barrier, inc=1, device_id=(p, side), device_id_type=MESH)
@@ -101,6 +100,16 @@
     def _():
         pl.semaphore_signal(
             barrier, inc=1, device_id=(jnp.maximum(p - LINE + 1, 0), q), device_id_type=MESH
+        )
+
+    for c in range(4):
+        for copy in loads(c):
+            copy.start()
+
+    def stores(i):
+        return (
+            pltpu.make_async_copy(phases.at[:, i], phases_out.at[:, i], store.at[i, 0]),
+            pltpu.make_async_copy(potentials.at[:, i], potentials_out.at[:, i], store.at[i, 1]),
         )
 
     def begin(i, carry):
@@ -351,6 +360,13 @@
         def _():
             run(odd, None, 1, first, last)
 
+            def write(j, c):
+                for copy in stores(j - 2 * TOTAL):
+                    copy.start()
+                return c
+
+            lax.fori_loop(first, last, write, 0)
+
     def iteration(n, carry):
         @pl.when((n >= GROUPS - 1) & (n - GROUPS + 1 < TOTAL))
         def _():
@@ -395,6 +411,13 @@
         return carry
 
     lax.fori_loop(1, TOTAL + GROUPS, iteration, 0)
+
+    def written(i, carry):
+        for copy in stores(i):
+            copy.wait()
+        return carry
+
+    lax.fori_loop(0, block, written, 0)
 
     @pl.when(p > 0)
     def _():
@@ -423,7 +446,6 @@
         block, rows, cols = labels.shape
         span = block + 2 * TOTAL + LEAD
         field = pltpu.VMEM((span, FIELDS, rows + 2 * HALO + 2 * PAD, cols), jnp.float32)
-        vmem = pl.BlockSpec(memory_space=pltpu.VMEM)
         hbm = pl.BlockSpec(memory_space=pltpu.HBM)
         smem = pl.BlockSpec(memory_space=pltpu.SMEM)
         return pl.pallas_call(
@@ -433,7 +455,7 @@
                 jax.ShapeDtypeStruct((2, block, rows, cols), jnp.float32),
             ),
             in_specs=[hbm] * 4 + [smem] * 5,
-            out_specs=(vmem, vmem),
+            out_specs=(hbm, hbm),
             scratch_shapes=[field, field] + [
                 pltpu.SemaphoreType.DMA((TOTAL, LEAD)),
                 pltpu.SemaphoreType.DMA((TOTAL, LEAD)),
@@ -449,6 +471,9 @@
                 pltpu.VMEM((2, block, rows, cols), jnp.float32),
                 pltpu.VMEM((ROUNDS, SHIFT, rows, cols), jnp.int32),
                 pltpu.SemaphoreType.DMA((13,)),
+                pltpu.VMEM((4, block, rows, cols), jnp.float32),
+                pltpu.VMEM((2, block, rows, cols), jnp.float32),
+                pltpu.SemaphoreType.DMA((block, 2)),
             ],
             compiler_params=pltpu.CompilerParams(
                 collective_id=0, has_side_effects=True, vmem_limit_bytes=60 << 20

time: 109 us -> 107 us (0.982); the launches traced: 107 us -> 107 us
  no operation moved by 1% of the time
where the time goes in v4:
time: 107 us
  Pallas kernels  103 us (96%)
  local copies, waits for them, and re-layouts  3.12 us (3%)
    pallas_call x1, Pallas kernels, on_device(): pl.pallas_call(functools.partial(kernel, peers, lats), out_shape=(jax.Sha...  103 us
    unnamed x4, local copies, waits for them, and re-layouts  3.12 us

profile of v4, /device:TPU:249, one launch (start us, length us, event | category | flops | bytes accessed | tf_op | source)
XLA Modules:
  0.0 106.8 jit_solution(3833929596103963945)
XLA Ops:
  0.6 103.0 %shard_map.104 = (f32[4,16,32,128]{3,2,1,0:T(8,128)}, f32[2,16,32,128]{3,2,1,0:T(8,128)}) custom-call(s32[16,32,128]{2,1,0:T(8,128)} %labels_in.1, f32[4,16,32,128]{3,2,1,0:T(8,128)} %rough_in.1, f32[2,16,32,128]{3,2,1,0:T(8,128)} %pot_in.1, s32[4,8,32,128]{3,2,1,0:T(8,128)} %melt_in.1, f32[4,3]{1,0:T(4,128)} %grad.1, f32[2,4]{1,0:T(2,128)} %bitcast.2, ...), custom_call_target="tpu_custom_call" | custom-call | tf_op jit(solution)/shard_map/pallas_call | solution.py:451
  103.7 0.0 copy-start
  103.7 2.3 %copy.13 = f32[4,16,32,128]{3,2,1,0:T(8,128)} copy(f32[4,16,32,128]{3,2,1,0:T(8,128)} %get-tuple-element.4) | data formatting | bytes 2097152
  106.0 0.0 copy-done
  106.0 0.8 copy.14
Async XLA Ops:
  103.7 2.3 %copy-start = (f32[2,16,32,128]{3,2,1,0:T(8,128)S(1)}, f32[2,16,32,128]{3,2,1,0:T(8,128)}, u32[]{:S(2)}) copy-start(f32[2,16,32,128]{3,2,1,0:T(8,128)} %get-tuple-element.5) | copy-start | bytes 1572868

commit v5 on v4

--- a/solution.py
+++ b/solution.py
@@ -201,8 +201,8 @@
     def own_copies(c):
         return halo_copies(even, 4 * c, 4, own_send.at[c], own_recv.at[c])
 
-    def side_copies(t, field):
-        return halo_copies(field, 2 * t + block, LEAD, x_send.at[t], x_recv.at[t])
+    def side_copies(t, field, count):
+        return halo_copies(field, 2 * t + block, count, x_send.at[t], x_recv.at[t])
 
     send_down(0, 0, even)
 
@@ -230,27 +230,42 @@
                     value = jnp.where(chosen == e, table[k, e], value)
                 field[2 * t + block + l, 3 + k, pl.ds(low, rows)] = value
 
+    def landed(t, l):
+        @pl.when(p < peers - 1)
+        def _():
+            down_copy(t, l, even).wait_recv()
+
     def arrive(t):
-        @pl.when(p < peers - 1)
-        def _():
-            for l in range(LEAD):
-                down_copy(t, l, even).wait_recv()
-
         for parity, field in ((0, even), (1, odd)):
             @pl.when((p == peers - 1) & (lax.rem(t, 2) == parity))
             def _():
                 melt(t, field)
 
-            @pl.when(lax.rem(t, 2) == parity)
-            def _():
-                for copy in side_copies(t, field):
+        landed(t, 0)
+        landed(t, 1)
+
+        @pl.when(t == TOTAL - 1)
+        def _():
+            for copy in side_copies(t, odd, LEAD - 1):
+                copy.start()
+
+        landed(t, 2)
+        for parity, field in ((0, even), (1, odd)):
+            @pl.when((t < TOTAL - 1) & (lax.rem(t, 2) == parity))
+            def _():
+                for copy in side_copies(t, field, LEAD):
                     copy.start()
 
     def sides_done(t):
+        @pl.when(t == TOTAL - 1)
+        def _():
+            for copy in side_copies(t, odd, LEAD - 1):
+                copy.wait()
+
         for parity, field in ((0, even), (1, odd)):
-            @pl.when(lax.rem(t, 2) == parity)
-            def _():
-                for copy in side_copies(t, field):
+            @pl.when((t < TOTAL - 1) & (lax.rem(t, 2) == parity))
+            def _():
+                for copy in side_copies(t, field, LEAD):
                     copy.wait()
 
     gr = [[DT * grad[a, i] for i in range(3)] for a in range(4)]

time: 107 us -> 107 us (level)
  no operation moved by 1% of the time
where the time goes in v5:
time: 107 us; the launch traced here: 106 us
  Pallas kernels  103 us (96%)
  local copies, waits for them, and re-layouts  3.12 us (3%)
    pallas_call x1, Pallas kernels, on_device(): pl.pallas_call(functools.partial(kernel, peers, lats), out_shape=(jax.Sha...  103 us
    unnamed x4, local copies, waits for them, and re-layouts  3.12 us

profile of v5, /device:TPU:249, one launch (start us, length us, event | category | flops | bytes accessed | tf_op | source)
XLA Modules:
  0.0 106.4 jit_solution(6448704973789941922)
XLA Ops:
  0.6 102.6 %shard_map.104 = (f32[4,16,32,128]{3,2,1,0:T(8,128)}, f32[2,16,32,128]{3,2,1,0:T(8,128)}) custom-call(s32[16,32,128]{2,1,0:T(8,128)} %labels_in.1, f32[4,16,32,128]{3,2,1,0:T(8,128)} %rough_in.1, f32[2,16,32,128]{3,2,1,0:T(8,128)} %pot_in.1, s32[4,8,32,128]{3,2,1,0:T(8,128)} %melt_in.1, f32[4,3]{1,0:T(4,128)} %grad.1, f32[2,4]{1,0:T(2,128)} %bitcast.2, ...), custom_call_target="tpu_custom_call" | custom-call | tf_op jit(solution)/shard_map/pallas_call | solution.py:466
  103.2 0.0 copy-start
  103.2 2.3 %copy.13 = f32[4,16,32,128]{3,2,1,0:T(8,128)} copy(f32[4,16,32,128]{3,2,1,0:T(8,128)} %get-tuple-element.4) | data formatting | bytes 2097152
  105.6 0.0 copy-done
  105.6 0.8 copy.14
Async XLA Ops:
  103.2 2.3 %copy-start = (f32[2,16,32,128]{3,2,1,0:T(8,128)S(1)}, f32[2,16,32,128]{3,2,1,0:T(8,128)}, u32[]{:S(2)}) copy-start(f32[2,16,32,128]{3,2,1,0:T(8,128)} %get-tuple-element.5) | copy-start | bytes 1572868
